TPU v7x, 32 devices: a whole 2x2x4 slice. The times are simulated.
32 devices in a mesh: ctx: 16 (over z, y, core), tp: 2 (over x).
Axes of the slice: x: 2, y: 2, z: 4, core: 2. Of those that a mesh axis runs over, the one named last changes fastest.
Arguments:
- queries: bfloat16 [2048, 2048], P('ctx', 'tp'), may hold values from -6 to 6
- keys_values: bfloat16 [2048, 256], P('ctx', 'tp'), may hold values from -6 to 6
- forward_out: bfloat16 [2048, 2048], P('ctx', 'tp'), may hold values from -6 to 6
- out_grad: bfloat16 [2048, 2048], P('ctx', 'tp'), may hold values from -6 to 6
- kv_weight: bfloat16 [14848, 256], P(None, 'tp'), may hold values from -3 to 3
- span_table: int32 [32], replicated, may hold values from 0 to 31, each once
Outputs:
- query_grad: bfloat16 [2048, 2048], P('ctx', 'tp')
- input_grad: bfloat16 [2048, 14848], P('ctx', 'tp')
Inputs may be any that keep to these rules, and one draw needn't show every extreme that they name: `span_table`: a permutation: every sequence block appears once.
All inputs are finite; a program needn't handle non-finite values.
Results may differ from a plain program's by a relative error of at most 0.0057.
Values may be sent and summed in bfloat16 or wider, within the bound.
A program may use at most 64 MiB of HBM per device.

v0:
```python
import jax
import jax.numpy as jnp
from jax import lax
from jax.sharding import PartitionSpec as P

HEAD = 64


softmax_scale = 0.125
masked_score = -1e30


def passed_along(value, axis, steps):
    count = lax.axis_size(axis)
    pairs = [(source, (source + steps) % count) for source in range(count)]
    return lax.ppermute(value, axis, pairs)


def key_positions(first_row, row_count, span_table, span_rows):
    row_ids = first_row + jnp.arange(row_count, dtype=jnp.int32)
    blocks = row_ids // span_rows
    onehot = blocks[:, None] == jnp.arange(span_table.shape[0], dtype=jnp.int32)[None, :]
    starts = jnp.sum(jnp.where(onehot, span_table[None, :], 0), axis=1)
    return starts * span_rows + row_ids % span_rows


def block_scores(query_heads, key_rows, query_pos, key_pos):
    scores = (
        jnp.einsum("qhd,kd->hqk", query_heads, key_rows, preferred_element_type=jnp.float32)
        * softmax_scale
    )
    visible = (key_pos[None, :] <= query_pos[:, None])[None]
    return (jnp.where(visible, scores, masked_score), visible)


def on_device(queries, keys_values, forward_out, out_grad, kv_weight, span_table):
    tokens = queries.shape[0]
    span_rows = tokens // 2
    head_count = queries.shape[1] // HEAD
    cycle_index = lax.axis_index("ctx")
    cycle_size = lax.axis_size("ctx")
    query_pos = key_positions(cycle_index * tokens, tokens, span_table, span_rows)
    query_heads = queries.reshape(tokens, head_count, HEAD)
    grad_heads = out_grad.reshape(tokens, head_count, HEAD)
    forward_heads = forward_out.reshape(tokens, head_count, HEAD)
    grad_dot = jnp.sum(grad_heads.astype(jnp.float32) * forward_heads.astype(jnp.float32), axis=2).T
    gathered = lax.all_gather(keys_values, "ctx", axis=0, tiled=True)
    total_rows = gathered.shape[0]
    block_rows = min(512, total_rows)
    block_ids = jnp.arange(total_rows // block_rows, dtype=jnp.int32)

    def stats_step(running, block_index):
        row_top, row_total = running
        first_row = block_index * block_rows
        rows_block = lax.dynamic_slice_in_dim(gathered, first_row, block_rows, 0)
        key_pos = key_positions(first_row, block_rows, span_table, span_rows)
        scores, visible = block_scores(query_heads, rows_block[:, :HEAD], query_pos, key_pos)
        new_top = jnp.maximum(row_top, jnp.max(scores, axis=2))
        block_total = jnp.sum(
            jnp.where(visible, jnp.exp(scores - new_top[:, :, None]), 0.0), axis=2
        )
        row_total = row_total * jnp.exp(row_top - new_top) + block_total
        return ((new_top, row_total), None)

    start_top = jnp.full((head_count, tokens), masked_score, jnp.float32)
    start_total = jnp.zeros((head_count, tokens), jnp.float32)
    (row_top, row_total), _ = lax.scan(stats_step, (start_top, start_total), block_ids)
    log_total = row_top + jnp.log(row_total)

    def key_grads(first_row, row_count):
        rows_block = lax.dynamic_slice_in_dim(gathered, first_row, row_count, 0)
        key_rows = rows_block[:, :HEAD]
        value_rows = rows_block[:, HEAD:]
        key_pos = key_positions(first_row, row_count, span_table, span_rows)
        scores, visible = block_scores(query_heads, key_rows, query_pos, key_pos)
        probabilities = jnp.where(visible, jnp.exp(scores - log_total[:, :, None]), 0.0)
        weights = probabilities.astype(jnp.bfloat16)
        dprobs = jnp.einsum(
            "qhd,kd->hqk", grad_heads, value_rows, preferred_element_type=jnp.float32
        )
        dscores = (probabilities * (dprobs - grad_dot[:, :, None])).astype(jnp.bfloat16)
        query_add = jnp.einsum("hqk,kd->qhd", dscores, key_rows, preferred_element_type=jnp.float32)
        key_add = (
            jnp.einsum("hqk,qhd->kd", dscores, query_heads, preferred_element_type=jnp.float32)
            * softmax_scale
        )
        value_add = jnp.einsum(
            "hqk,qhd->kd", weights, grad_heads, preferred_element_type=jnp.float32
        )
        return (query_add, jnp.concatenate([key_add, value_add], axis=1))

    query_start = jnp.zeros((tokens, head_count, HEAD), jnp.float32)

    def travel_step(turn_index, running):
        query_sum, carried = running
        owner_block = (cycle_index - turn_index) % cycle_size
        query_add, own_add = key_grads(owner_block * tokens, tokens)
        carried = passed_along(carried + own_add, "ctx", 1)
        return (query_sum + query_add, carried)

    carried_start = jnp.zeros((tokens, 2 * HEAD), jnp.float32)
    query_sum, kv_sum = lax.fori_loop(0, cycle_size, travel_step, (query_start, carried_start))
    query_grad = (query_sum * softmax_scale).astype(jnp.bfloat16).reshape(tokens, head_count * HEAD)
    kv_grad = kv_sum.astype(jnp.bfloat16)
    partial_terms = lax.dot_general(
        kv_grad, kv_weight, (((1,), (1,)), ((), ())), preferred_element_type=jnp.float32
    )
    input_grad = lax.psum_scatter(partial_terms, "tp", scatter_dimension=1, tiled=True)
    return (query_grad, input_grad.astype(jnp.bfloat16))


def solution(mesh):
    placed = (P("ctx", "tp"), P("ctx", "tp"), P("ctx", "tp"), P("ctx", "tp"), P(None, "tp"), P())
    return jax.shard_map(
        on_device,
        mesh=mesh,
        in_specs=placed,
        out_specs=(P("ctx", "tp"), P("ctx", "tp")),
        check_vma=False,
    )
```

profile of v0, /device:TPU:0, one launch (start us, length us, event | category | flops | bytes accessed | tf_op | source)
XLA Modules:
  0.0 296.8 jit_solution(6517733631723495582)
XLA Ops:
  8.0 0.9 copy.27
  8.9 1.1 copy.29
  10.0 1.1 copy.28
  11.1 24.6 %all_gather.3 = bf16[2048,128]{0,1:T(8,128)(2,1)S(1)} all-gather(bf16[128,128]{0,1:T(8,128)(2,1)S(1)} %copy.27), channel_id=1, replica_groups=mesh['ctx'=16,'tp'=2] {'ctx'}, dimensions={0}, use_global_device_ids=true | all-gather | bytes 557056 | tf_op jit(solution)/shard_map/all_gather | solution.py:47
  35.7 16.4 %while.34 = (s32[]{:T(128)}, f32[16,128]{1,0:T(8,128)S(1)}, f32[16,128]{1,0:T(8,128)S(1)}, s32[4]{0:T(128)S(1)}, s32[32]{0:T(128)}, /*index=5*/s32[128]{0:T(128)...) while((s32[]{:T(128)}, f32[16,128]{1,0:T(8,128)S(1)}, ...), condition=%wide.region_5.6_spmd.clone, body=%wide.region_1.5_spmd.clone.sunk | while | flops 142746112 | bytes 9032526 | solution.py:67
  38.0 0.7 fusion.51
  38.8 1.0 select_reduce_fusion.8
  42.9 1.0 select_reduce_fusion.8
  46.2 0.7 fusion.51
  47.0 1.0 select_reduce_fusion.8
  51.1 1.0 select_reduce_fusion.8
  52.4 139.1 %while.35 = (s32[]{:T(128)}, f32[128,16,64]{0,2,1:T(8,128)S(1)}, f32[128,128]{0,1:T(8,128)S(1)}, s32[]{:T(128)}, bf16[2048,128]{0,1:T(8,128)(2,1)S(1)}, /*index=...) while((s32[]{:T(128)}, f32[128,16,64]{0,2,1:T(8,128)S(1)}, ...), condition=%wide.region_9.10_spmd.clone, body=%wide.region_7.9_spmd.clone.sunk | while | flops 170204816 | bytes 7442466 | solution.py:102
  55.4 5.7 %collective-permute-done = f32[128,128]{0,1:T(8,128)S(1)} collective-permute-done((f32[128,128]{0,1:T(8,128)S(1)}, f32[128,128]{0,1:T(8,128)S(1)}, u32[]{:S(2)}, u32[]{:S(2)}) %collective-permute-start) | collective-permute-done | bytes 65568 | tf_op jit(solution)/shard_map/while/body/eval_jaxpr/ppermute | solution.py:16
  63.7 6.1 %collective-permute-done = f32[128,128]{0,1:T(8,128)S(1)} collective-permute-done((f32[128,128]{0,1:T(8,128)S(1)}, f32[128,128]{0,1:T(8,128)S(1)}, u32[]{:S(2)}, u32[]{:S(2)}) %collective-permute-start) | collective-permute-done | bytes 65568 | tf_op jit(solution)/shard_map/while/body/eval_jaxpr/ppermute | solution.py:16
  72.4 6.1 %collective-permute-done = f32[128,128]{0,1:T(8,128)S(1)} collective-permute-done((f32[128,128]{0,1:T(8,128)S(1)}, f32[128,128]{0,1:T(8,128)S(1)}, u32[]{:S(2)}, u32[]{:S(2)}) %collective-permute-start) | collective-permute-done | bytes 65568 | tf_op jit(solution)/shard_map/while/body/eval_jaxpr/ppermute | solution.py:16
  81.1 6.1 %collective-permute-done = f32[128,128]{0,1:T(8,128)S(1)} collective-permute-done((f32[128,128]{0,1:T(8,128)S(1)}, f32[128,128]{0,1:T(8,128)S(1)}, u32[]{:S(2)}, u32[]{:S(2)}) %collective-permute-start) | collective-permute-done | bytes 65568 | tf_op jit(solution)/shard_map/while/body/eval_jaxpr/ppermute | solution.py:16
  89.8 6.1 %collective-permute-done = f32[128,128]{0,1:T(8,128)S(1)} collective-permute-done((f32[128,128]{0,1:T(8,128)S(1)}, f32[128,128]{0,1:T(8,128)S(1)}, u32[]{:S(2)}, u32[]{:S(2)}) %collective-permute-start) | collective-permute-done | bytes 65568 | tf_op jit(solution)/shard_map/while/body/eval_jaxpr/ppermute | solution.py:16
  98.5 6.1 %collective-permute-done = f32[128,128]{0,1:T(8,128)S(1)} collective-permute-done((f32[128,128]{0,1:T(8,128)S(1)}, f32[128,128]{0,1:T(8,128)S(1)}, u32[]{:S(2)}, u32[]{:S(2)}) %collective-permute-start) | collective-permute-done | bytes 65568 | tf_op jit(solution)/shard_map/while/body/eval_jaxpr/ppermute | solution.py:16
  107.2 6.1 %collective-permute-done = f32[128,128]{0,1:T(8,128)S(1)} collective-permute-done((f32[128,128]{0,1:T(8,128)S(1)}, f32[128,128]{0,1:T(8,128)S(1)}, u32[]{:S(2)}, u32[]{:S(2)}) %collective-permute-start) | collective-permute-done | bytes 65568 | tf_op jit(solution)/shard_map/while/body/eval_jaxpr/ppermute | solution.py:16
  115.9 6.1 %collective-permute-done = f32[128,128]{0,1:T(8,128)S(1)} collective-permute-done((f32[128,128]{0,1:T(8,128)S(1)}, f32[128,128]{0,1:T(8,128)S(1)}, u32[]{:S(2)}, u32[]{:S(2)}) %collective-permute-start) | collective-permute-done | bytes 65568 | tf_op jit(solution)/shard_map/while/body/eval_jaxpr/ppermute | solution.py:16
  124.6 6.1 %collective-permute-done = f32[128,128]{0,1:T(8,128)S(1)} collective-permute-done((f32[128,128]{0,1:T(8,128)S(1)}, f32[128,128]{0,1:T(8,128)S(1)}, u32[]{:S(2)}, u32[]{:S(2)}) %collective-permute-start) | collective-permute-done | bytes 65568 | tf_op jit(solution)/shard_map/while/body/eval_jaxpr/ppermute | solution.py:16
  133.3 6.1 %collective-permute-done = f32[128,128]{0,1:T(8,128)S(1)} collective-permute-done((f32[128,128]{0,1:T(8,128)S(1)}, f32[128,128]{0,1:T(8,128)S(1)}, u32[]{:S(2)}, u32[]{:S(2)}) %collective-permute-start) | collective-permute-done | bytes 65568 | tf_op jit(solution)/shard_map/while/body/eval_jaxpr/ppermute | solution.py:16
  142.0 6.1 %collective-permute-done = f32[128,128]{0,1:T(8,128)S(1)} collective-permute-done((f32[128,128]{0,1:T(8,128)S(1)}, f32[128,128]{0,1:T(8,128)S(1)}, u32[]{:S(2)}, u32[]{:S(2)}) %collective-permute-start) | collective-permute-done | bytes 65568 | tf_op jit(solution)/shard_map/while/body/eval_jaxpr/ppermute | solution.py:16
  150.7 6.1 %collective-permute-done = f32[128,128]{0,1:T(8,128)S(1)} collective-permute-done((f32[128,128]{0,1:T(8,128)S(1)}, f32[128,128]{0,1:T(8,128)S(1)}, u32[]{:S(2)}, u32[]{:S(2)}) %collective-permute-start) | collective-permute-done | bytes 65568 | tf_op jit(solution)/shard_map/while/body/eval_jaxpr/ppermute | solution.py:16
  159.3 6.1 %collective-permute-done = f32[128,128]{0,1:T(8,128)S(1)} collective-permute-done((f32[128,128]{0,1:T(8,128)S(1)}, f32[128,128]{0,1:T(8,128)S(1)}, u32[]{:S(2)}, u32[]{:S(2)}) %collective-permute-start) | collective-permute-done | bytes 65568 | tf_op jit(solution)/shard_map/while/body/eval_jaxpr/ppermute | solution.py:16
  168.0 6.1 %collective-permute-done = f32[128,128]{0,1:T(8,128)S(1)} collective-permute-done((f32[128,128]{0,1:T(8,128)S(1)}, f32[128,128]{0,1:T(8,128)S(1)}, u32[]{:S(2)}, u32[]{:S(2)}) %collective-permute-start) | collective-permute-done | bytes 65568 | tf_op jit(solution)/shard_map/while/body/eval_jaxpr/ppermute | solution.py:16
  176.7 6.1 %collective-permute-done = f32[128,128]{0,1:T(8,128)S(1)} collective-permute-done((f32[128,128]{0,1:T(8,128)S(1)}, f32[128,128]{0,1:T(8,128)S(1)}, u32[]{:S(2)}, u32[]{:S(2)}) %collective-permute-start) | collective-permute-done | bytes 65568 | tf_op jit(solution)/shard_map/while/body/eval_jaxpr/ppermute | solution.py:16
  185.4 6.1 %collective-permute-done = f32[128,128]{0,1:T(8,128)S(1)} collective-permute-done((f32[128,128]{0,1:T(8,128)S(1)}, f32[128,128]{0,1:T(8,128)S(1)}, u32[]{:S(2)}, u32[]{:S(2)}) %collective-permute-start) | collective-permute-done | bytes 65568 | tf_op jit(solution)/shard_map/while/body/eval_jaxpr/ppermute | solution.py:16
  191.5 6.3 %fusion.22 = f32[128,14848]{1,0:T(8,128)} fusion(bf16[14848,128]{1,0:T(8,128)(2,1)} %param.14, f32[128,128]{0,1:T(8,128)S(1)} %get-tuple-element.415), kind=kOutput, calls=%fused_computation.56 | convolution fusion | flops 486555648 | bytes 11468800 | tf_op jit(solution)/shard_map/dot_general | solution.py:105
  197.8 0.9 copy.31
  198.7 87.8 %reduce-scatter.2.cloned.1.call-done = f32[128,7424]{1,0:T(8,128)} async-done(((f32[128,14848]{1,0:T(8,128)}), f32[128,7424]{1,0:T(8,128)}) %reduce-scatter.2.cloned.1.call-update) | async-done | bytes 3801104 | tf_op jit(solution)/shard_map/reduce_scatter | solution.py:108
  286.5 3.5 %convert_element_type.45 = bf16[128,7424]{1,0:T(8,128)(2,1)} convert(f32[128,7424]{1,0:T(8,128)} %reduce-scatter.2.cloned.1.call-done) | non-fusion elementwise | flops 950272 | bytes 5701632 | tf_op jit(solution)/shard_map/convert_element_type | solution.py:109
  (226 shorter events, 50.1 us)
Async XLA Ops:
  7.2 279.3 %reduce-scatter.2.cloned.1.call-start = ((), (), s32[]{:S(2)}) async-start(), calls=%async_computation.1 | async-start | bytes 11403264 | tf_op jit(solution)/shard_map/reduce_scatter | solution.py:108
  35.7 16.4 %copy-start = (bf16[128,1024]{1,0:T(8,128)(2,1)S(1)}, bf16[128,1024]{1,0:T(8,128)(2,1)}, u32[]{:S(2)}) copy-start(bf16[128,1024]{1,0:T(8,128)(2,1)} %param.12) | copy-start | bytes 786436
  54.7 6.4 %collective-permute-start = (f32[128,128]{0,1:T(8,128)S(1)}, f32[128,128]{0,1:T(8,128)S(1)}, u32[]{:S(2)}, u32[]{:S(2)}) collective-permute-start(f32[128,128]{0,1:T(8,128)S(1)} %maximum_add_fusion.2), channel_id=1, source_target_pairs={{0,2},{2,4},{4,6},{6,8},{8,10},{10,12},{12,14},{14,16},{16,18},{18... | collective-permute-start | bytes 196616 | tf_op jit(solution)/shard_map/while/body/eval_jaxpr/ppermute | solution.py:16
  63.4 6.4 %collective-permute-start = (f32[128,128]{0,1:T(8,128)S(1)}, f32[128,128]{0,1:T(8,128)S(1)}, u32[]{:S(2)}, u32[]{:S(2)}) collective-permute-start(f32[128,128]{0,1:T(8,128)S(1)} %maximum_add_fusion.2), channel_id=1, source_target_pairs={{0,2},{2,4},{4,6},{6,8},{8,10},{10,12},{12,14},{14,16},{16,18},{18... | collective-permute-start | bytes 196616 | tf_op jit(solution)/shard_map/while/body/eval_jaxpr/ppermute | solution.py:16
  72.1 6.4 %collective-permute-start = (f32[128,128]{0,1:T(8,128)S(1)}, f32[128,128]{0,1:T(8,128)S(1)}, u32[]{:S(2)}, u32[]{:S(2)}) collective-permute-start(f32[128,128]{0,1:T(8,128)S(1)} %maximum_add_fusion.2), channel_id=1, source_target_pairs={{0,2},{2,4},{4,6},{6,8},{8,10},{10,12},{12,14},{14,16},{16,18},{18... | collective-permute-start | bytes 196616 | tf_op jit(solution)/shard_map/while/body/eval_jaxpr/ppermute | solution.py:16
  80.8 6.4 %collective-permute-start = (f32[128,128]{0,1:T(8,128)S(1)}, f32[128,128]{0,1:T(8,128)S(1)}, u32[]{:S(2)}, u32[]{:S(2)}) collective-permute-start(f32[128,128]{0,1:T(8,128)S(1)} %maximum_add_fusion.2), channel_id=1, source_target_pairs={{0,2},{2,4},{4,6},{6,8},{8,10},{10,12},{12,14},{14,16},{16,18},{18... | collective-permute-start | bytes 196616 | tf_op jit(solution)/shard_map/while/body/eval_jaxpr/ppermute | solution.py:16
  89.4 6.4 %collective-permute-start = (f32[128,128]{0,1:T(8,128)S(1)}, f32[128,128]{0,1:T(8,128)S(1)}, u32[]{:S(2)}, u32[]{:S(2)}) collective-permute-start(f32[128,128]{0,1:T(8,128)S(1)} %maximum_add_fusion.2), channel_id=1, source_target_pairs={{0,2},{2,4},{4,6},{6,8},{8,10},{10,12},{12,14},{14,16},{16,18},{18... | collective-permute-start | bytes 196616 | tf_op jit(solution)/shard_map/while/body/eval_jaxpr/ppermute | solution.py:16
  98.1 6.4 %collective-permute-start = (f32[128,128]{0,1:T(8,128)S(1)}, f32[128,128]{0,1:T(8,128)S(1)}, u32[]{:S(2)}, u32[]{:S(2)}) collective-permute-start(f32[128,128]{0,1:T(8,128)S(1)} %maximum_add_fusion.2), channel_id=1, source_target_pairs={{0,2},{2,4},{4,6},{6,8},{8,10},{10,12},{12,14},{14,16},{16,18},{18... | collective-permute-start | bytes 196616 | tf_op jit(solution)/shard_map/while/body/eval_jaxpr/ppermute | solution.py:16
  106.8 6.4 %collective-permute-start = (f32[128,128]{0,1:T(8,128)S(1)}, f32[128,128]{0,1:T(8,128)S(1)}, u32[]{:S(2)}, u32[]{:S(2)}) collective-permute-start(f32[128,128]{0,1:T(8,128)S(1)} %maximum_add_fusion.2), channel_id=1, source_target_pairs={{0,2},{2,4},{4,6},{6,8},{8,10},{10,12},{12,14},{14,16},{16,18},{18... | collective-permute-start | bytes 196616 | tf_op jit(solution)/shard_map/while/body/eval_jaxpr/ppermute | solution.py:16
  115.5 6.4 %collective-permute-start = (f32[128,128]{0,1:T(8,128)S(1)}, f32[128,128]{0,1:T(8,128)S(1)}, u32[]{:S(2)}, u32[]{:S(2)}) collective-permute-start(f32[128,128]{0,1:T(8,128)S(1)} %maximum_add_fusion.2), channel_id=1, source_target_pairs={{0,2},{2,4},{4,6},{6,8},{8,10},{10,12},{12,14},{14,16},{16,18},{18... | collective-permute-start | bytes 196616 | tf_op jit(solution)/shard_map/while/body/eval_jaxpr/ppermute | solution.py:16
  124.2 6.4 %collective-permute-start = (f32[128,128]{0,1:T(8,128)S(1)}, f32[128,128]{0,1:T(8,128)S(1)}, u32[]{:S(2)}, u32[]{:S(2)}) collective-permute-start(f32[128,128]{0,1:T(8,128)S(1)} %maximum_add_fusion.2), channel_id=1, source_target_pairs={{0,2},{2,4},{4,6},{6,8},{8,10},{10,12},{12,14},{14,16},{16,18},{18... | collective-permute-start | bytes 196616 | tf_op jit(solution)/shard_map/while/body/eval_jaxpr/ppermute | solution.py:16
  132.9 6.4 %collective-permute-start = (f32[128,128]{0,1:T(8,128)S(1)}, f32[128,128]{0,1:T(8,128)S(1)}, u32[]{:S(2)}, u32[]{:S(2)}) collective-permute-start(f32[128,128]{0,1:T(8,128)S(1)} %maximum_add_fusion.2), channel_id=1, source_target_pairs={{0,2},{2,4},{4,6},{6,8},{8,10},{10,12},{12,14},{14,16},{16,18},{18... | collective-permute-start | bytes 196616 | tf_op jit(solution)/shard_map/while/body/eval_jaxpr/ppermute | solution.py:16
  141.6 6.4 %collective-permute-start = (f32[128,128]{0,1:T(8,128)S(1)}, f32[128,128]{0,1:T(8,128)S(1)}, u32[]{:S(2)}, u32[]{:S(2)}) collective-permute-start(f32[128,128]{0,1:T(8,128)S(1)} %maximum_add_fusion.2), channel_id=1, source_target_pairs={{0,2},{2,4},{4,6},{6,8},{8,10},{10,12},{12,14},{14,16},{16,18},{18... | collective-permute-start | bytes 196616 | tf_op jit(solution)/shard_map/while/body/eval_jaxpr/ppermute | solution.py:16
  150.3 6.4 %collective-permute-start = (f32[128,128]{0,1:T(8,128)S(1)}, f32[128,128]{0,1:T(8,128)S(1)}, u32[]{:S(2)}, u32[]{:S(2)}) collective-permute-start(f32[128,128]{0,1:T(8,128)S(1)} %maximum_add_fusion.2), channel_id=1, source_target_pairs={{0,2},{2,4},{4,6},{6,8},{8,10},{10,12},{12,14},{14,16},{16,18},{18... | collective-permute-start | bytes 196616 | tf_op jit(solution)/shard_map/while/body/eval_jaxpr/ppermute | solution.py:16
  159.0 6.4 %collective-permute-start = (f32[128,128]{0,1:T(8,128)S(1)}, f32[128,128]{0,1:T(8,128)S(1)}, u32[]{:S(2)}, u32[]{:S(2)}) collective-permute-start(f32[128,128]{0,1:T(8,128)S(1)} %maximum_add_fusion.2), channel_id=1, source_target_pairs={{0,2},{2,4},{4,6},{6,8},{8,10},{10,12},{12,14},{14,16},{16,18},{18... | collective-permute-start | bytes 196616 | tf_op jit(solution)/shard_map/while/body/eval_jaxpr/ppermute | solution.py:16
  167.7 6.4 %collective-permute-start = (f32[128,128]{0,1:T(8,128)S(1)}, f32[128,128]{0,1:T(8,128)S(1)}, u32[]{:S(2)}, u32[]{:S(2)}) collective-permute-start(f32[128,128]{0,1:T(8,128)S(1)} %maximum_add_fusion.2), channel_id=1, source_target_pairs={{0,2},{2,4},{4,6},{6,8},{8,10},{10,12},{12,14},{14,16},{16,18},{18... | collective-permute-start | bytes 196616 | tf_op jit(solution)/shard_map/while/body/eval_jaxpr/ppermute | solution.py:16
  176.4 6.4 %collective-permute-start = (f32[128,128]{0,1:T(8,128)S(1)}, f32[128,128]{0,1:T(8,128)S(1)}, u32[]{:S(2)}, u32[]{:S(2)}) collective-permute-start(f32[128,128]{0,1:T(8,128)S(1)} %maximum_add_fusion.2), channel_id=1, source_target_pairs={{0,2},{2,4},{4,6},{6,8},{8,10},{10,12},{12,14},{14,16},{16,18},{18... | collective-permute-start | bytes 196616 | tf_op jit(solution)/shard_map/while/body/eval_jaxpr/ppermute | solution.py:16
  185.0 6.4 %collective-permute-start = (f32[128,128]{0,1:T(8,128)S(1)}, f32[128,128]{0,1:T(8,128)S(1)}, u32[]{:S(2)}, u32[]{:S(2)}) collective-permute-start(f32[128,128]{0,1:T(8,128)S(1)} %maximum_add_fusion.2), channel_id=1, source_target_pairs={{0,2},{2,4},{4,6},{6,8},{8,10},{10,12},{12,14},{14,16},{16,18},{18... | collective-permute-start | bytes 196616 | tf_op jit(solution)/shard_map/while/body/eval_jaxpr/ppermute | solution.py:16
Sparse Core Ops, SparseCore 0:
  197.9 88.5 reduce-scatter.1
where the time goes:
time: 297 us
  waiting for transfers between devices  185 us (62%)
  matrix products  35.3 us (12%)
  other arithmetic  25.9 us (9%)
  blocking collectives  24.6 us (8%)
  between operations  14.1 us (5%)
  local copies, waits for them, and re-layouts  6.78 us (2%)
  loops' own time  4.22 us (1%)
    ppermute x16, waiting for transfers between devices, passed_along(): return lax.ppermute(value, axis, pairs)  96.8 us
    reduce_scatter x1, waiting for transfers between devices, on_device(): lax.psum_scatter(partial_terms, 'tp', scatter_dimension=1, tiled=True)  87.8 us
    all_gather x1, blocking collectives, on_device(): gathered = lax.all_gather(keys_values, 'ctx', axis=0, tiled=True)  24.6 us
    reduce_sum x21, other arithmetic, key_positions(): starts = jnp.sum(jnp.where(onehot, span_table[None, :], 0), axis=1)  15.7 us
    dot_general x20, matrix products, block_scores(): jnp.einsum('qhd,kd->hqk', query_heads, key_rows, preferred_element_type=j...  9.62 us
    dot_general x1, matrix products, on_device(): lax.dot_general(kv_grad, kv_weight, (((1,), (1,)), ((), ())), preferred_e...  6.27 us
  transfers between devices with their start and end apart: 17, of which 17 were waited for; matrix products, arithmetic and copies ran while one was open for 2% of the time, Pallas kernels for 0%

commit v1 on v0

v1 whole, which is shorter than its diff:
```python
import jax
import jax.numpy as jnp
from jax import lax
from jax.experimental import pallas as pl
from jax.experimental.pallas import tpu as pltpu
from jax.sharding import PartitionSpec as P

HEAD = 64
CHUNK_HEADS = 8
KEY_TILE = 256
softmax_scale = 0.125
log2_e = 1.4426950408889634
hidden = -1e30

NT = (((1,), (1,)), ((), ()))
NN = (((1,), (0,)), ((), ()))


def dot(a, b, dims=NN):
    return lax.dot_general(a, b, dims, preferred_element_type=jnp.float32)


def spread_queries(table_ref, first_span, half, q_ref, do_ref, fo_ref, qx, qs, dox):
    span_rows = q_ref.shape[0] // 2
    heads = q_ref.shape[1] // HEAD
    span = table_ref[first_span + half]
    row = lax.broadcasted_iota(jnp.int32, (span_rows, 2 * HEAD), 0)
    col = lax.broadcasted_iota(jnp.int32, (span_rows, 2 * HEAD), 1)
    blocked = jnp.where(col < HEAD, col - row, col - HEAD - span) > 0
    mask_cols = jnp.where(blocked, hidden, 0.0).astype(jnp.bfloat16)
    lane = lax.broadcasted_iota(jnp.int32, (span_rows, HEAD), 1)
    rows = pl.ds(half * span_rows, span_rows)
    for head in range(heads):
        pair = pl.ds(head // 2 * 2 * HEAD, 2 * HEAD)
        low = head % 2 * HEAD
        at = pl.ds((half * heads + head) * span_rows, span_rows)
        query = q_ref[rows, pair].astype(jnp.float32)[:, low:low + HEAD]
        grad = do_ref[rows, pair].astype(jnp.float32)[:, low:low + HEAD]
        forward = fo_ref[rows, pair].astype(jnp.float32)[:, low:low + HEAD]
        scaled = query * (softmax_scale * log2_e)
        top = scaled.astype(jnp.bfloat16).astype(jnp.float32)
        qx[at, 0:2 * HEAD] = jnp.concatenate([top, scaled - top], axis=1).astype(jnp.bfloat16)
        qx[at, 2 * HEAD:4 * HEAD] = mask_cols
        qs[at, :] = query.astype(jnp.bfloat16)
        left = -jnp.sum(grad * forward, axis=1, keepdims=True)
        tail = jnp.zeros((span_rows, HEAD), jnp.float32)
        for place in range(3):
            part = left.astype(jnp.bfloat16).astype(jnp.float32)
            tail = jnp.where(lane == place, part, tail)
            left = left - part
        dox[at, :] = jnp.concatenate([grad, tail], axis=1).astype(jnp.bfloat16)


def spread_keys(table_ref, first_span, first_row, block, kx, kt, vx):
    rows = block.shape[0]
    span_rows = rows // 2
    wide = block.astype(jnp.float32)
    key, value = wide[:, :HEAD], wide[:, HEAD:]
    lane = lax.broadcasted_iota(jnp.int32, (rows, HEAD), 1)
    ones = jnp.where(lane < 3, 1.0, 0.0)
    at = pl.ds(first_row, rows)
    vx[at, :] = jnp.concatenate([value, ones], axis=1).astype(jnp.bfloat16)
    eye = (
        lax.broadcasted_iota(jnp.int32, (HEAD, HEAD), 0)
        == lax.broadcasted_iota(jnp.int32, (HEAD, HEAD), 1)
    ).astype(jnp.bfloat16)
    kt[:, at] = dot(eye, key.astype(jnp.bfloat16), NT).astype(jnp.bfloat16)
    twice = jnp.concatenate([key, key], axis=1).astype(jnp.bfloat16)
    row = lax.broadcasted_iota(jnp.int32, (rows, 2 * HEAD), 0)
    col = lax.broadcasted_iota(jnp.int32, (rows, 2 * HEAD), 1)
    span_index = first_row // span_rows
    span = jnp.where(row < span_rows, table_ref[span_index], table_ref[span_index + 1])
    inner = jnp.where(row < span_rows, row, row - span_rows)
    for half in range(2):
        own = table_ref[first_span + half]
        wanted = jnp.where(col < HEAD, jnp.where(span == own, inner, -1), span + HEAD)
        kx[half, at, 0:2 * HEAD] = twice
        kx[half, at, 2 * HEAD:4 * HEAD] = jnp.where(wanted == col, 1.0, 0.0).astype(jnp.bfloat16)


def attention(chunk_count, chunk_rows, total_rows, span_rows, kx, kt, vx, qx, qs, dox, score, dk, dv, dq_ref):
    tiles = total_rows // KEY_TILE
    heads = dq_ref.shape[1] // HEAD

    def chunk_at(chunk):
        return pl.ds(chunk * chunk_rows, chunk_rows)

    def score_tile(chunk, tile, top):
        at = pl.ds(tile * KEY_TILE, KEY_TILE)
        half = chunk * 2 // chunk_count
        s = dot(kx[half, at, :], qx[chunk_at(chunk), :], NT)
        score[chunk % 2, at, :] = s
        return jnp.maximum(top, jnp.max(s.reshape(KEY_TILE // 8, 8, chunk_rows), axis=0))

    def exp_tile(chunk, tile, peak, total):
        at = pl.ds(tile * KEY_TILE, KEY_TILE)
        e = jnp.exp2(score[chunk % 2, at, :] - peak)
        score[chunk % 2, at, :] = e
        return total + jnp.sum(e.reshape(KEY_TILE // 8, 8, chunk_rows), axis=0)

    top_start = jnp.full((8, chunk_rows), hidden, jnp.float32)
    zero = jnp.zeros((8, chunk_rows), jnp.float32)
    top = lax.fori_loop(0, tiles, lambda tile, top: score_tile(0, tile, top), top_start)
    for chunk in range(chunk_count):
        peak = jnp.max(top, axis=0, keepdims=True)

        def first(tile, running, chunk=chunk, peak=peak):
            top, total = running
            if chunk + 1 < chunk_count:
                top = score_tile(chunk + 1, tile, top)
            return top, exp_tile(chunk, tile, peak, total)

        top, total = lax.fori_loop(0, tiles, first, (top_start, zero))
        inverse = 1.0 / jnp.sum(total, axis=0, keepdims=True)

        def second(tile, dqt, chunk=chunk, inverse=inverse):
            at = pl.ds(pl.multiple_of(tile * KEY_TILE, KEY_TILE), KEY_TILE)
            probs = score[chunk % 2, at, :] * inverse
            dprobs = dot(vx[at, :], dox[chunk_at(chunk), :], NT)
            dscores = (probs * dprobs).astype(jnp.bfloat16)
            dv_add = dot(probs.astype(jnp.bfloat16), dox[chunk_at(chunk), :])[:, :HEAD]
            dk_add = dot(dscores, qs[chunk_at(chunk), :])
            if chunk == 0:
                dv[at, :] = dv_add
                dk[at, :] = dk_add
            else:
                dv[at, :] += dv_add
                dk[at, :] += dk_add
            return dqt + dot(kt[:, at], dscores)

        dqt = lax.fori_loop(0, tiles, second, jnp.zeros((HEAD, chunk_rows), jnp.float32))
        dq = (dqt * softmax_scale).T
        half = chunk * 2 // chunk_count
        first_head = chunk * CHUNK_HEADS % heads
        for pair in range(CHUNK_HEADS // 2):
            parts = [
                dq[(2 * pair + side) * span_rows:(2 * pair + side + 1) * span_rows, :]
                for side in range(2)
            ]
            dq_ref[
                pl.ds(half * span_rows, span_rows),
                pl.ds((first_head + 2 * pair) * HEAD, 2 * HEAD),
            ] = jnp.concatenate(parts, axis=1).astype(jnp.bfloat16)


def attention_kernel(table_ref, q_ref, do_ref, fo_ref, kv_ref, dq_ref, dkv_ref, qx, qs, dox, kx, kt, vx, score, dk, dv):
    tokens = q_ref.shape[0]
    total_rows = kv_ref.shape[0]
    first_span = lax.axis_index("ctx") * 2
    for half in range(2):
        spread_queries(table_ref, first_span, half, q_ref, do_ref, fo_ref, qx, qs, dox)

    @pl.loop(0, total_rows // tokens)
    def _(owner):
        first_row = pl.multiple_of(owner * tokens, tokens)
        spread_keys(table_ref, first_span, first_row, kv_ref[pl.ds(first_row, tokens), :], kx, kt, vx)

    chunk_rows = CHUNK_HEADS * tokens // 2
    chunk_count = qx.shape[0] // chunk_rows
    attention(chunk_count, chunk_rows, total_rows, tokens // 2, kx, kt, vx, qx, qs, dox, score, dk, dv, dq_ref)
    dkv_ref[...] = jnp.concatenate([dk[...] * softmax_scale, dv[...]], axis=1)


def attention_scratch(tokens, heads, total_rows):
    rows = tokens * heads
    chunk_rows = CHUNK_HEADS * tokens // 2
    return [
        pltpu.VMEM((rows, 4 * HEAD), jnp.bfloat16),
        pltpu.VMEM((rows, HEAD), jnp.bfloat16),
        pltpu.VMEM((rows, 2 * HEAD), jnp.bfloat16),
        pltpu.VMEM((2, total_rows, 4 * HEAD), jnp.bfloat16),
        pltpu.VMEM((HEAD, total_rows), jnp.bfloat16),
        pltpu.VMEM((total_rows, 2 * HEAD), jnp.bfloat16),
        pltpu.VMEM((2, total_rows, chunk_rows), jnp.float32),
        pltpu.VMEM((total_rows, HEAD), jnp.float32),
        pltpu.VMEM((total_rows, HEAD), jnp.float32),
    ]


def on_device(queries, keys_values, forward_out, out_grad, kv_weight, span_table):
    tokens = queries.shape[0]
    heads = queries.shape[1] // HEAD
    tp_size = lax.axis_size("tp")
    ctx_size = lax.axis_size("ctx")
    tp_index = lax.axis_index("tp")
    core = lax.axis_index("ctx") % 2
    total_rows = tokens * ctx_size
    features = kv_weight.shape[0] // tp_size
    share = features // 2
    weights = []
    for step in range(1, tp_size):
        target = (tp_index + step) % tp_size
        piece = lax.dynamic_slice_in_dim(kv_weight, target * features + core * share, share, 0)
        mine = lax.ppermute(piece, "tp", [(s, (s + step) % tp_size) for s in range(tp_size)])
        mate = lax.ppermute(mine, "ctx", [(s, s ^ 1) for s in range(ctx_size)])
        low = jnp.where(core == 0, mine, mate)
        high = jnp.where(core == 0, mate, mine)
        weights.append(jnp.concatenate([low, high], axis=0))
    gathered = lax.all_gather(keys_values, "ctx", axis=0, tiled=True)
    vmem = pl.BlockSpec(memory_space=pltpu.VMEM)
    query_grad, kv_terms = pl.pallas_call(
        attention_kernel,
        out_shape=(
            jax.ShapeDtypeStruct(queries.shape, jnp.bfloat16),
            jax.ShapeDtypeStruct((total_rows, 2 * HEAD), jnp.float32),
        ),
        in_specs=[pl.BlockSpec(memory_space=pltpu.SMEM)] + [vmem] * 4,
        out_specs=(vmem, vmem),
        scratch_shapes=attention_scratch(tokens, heads, total_rows),
        compiler_params=pltpu.CompilerParams(vmem_limit_bytes=56 * 2**20),
        cost_estimate=pl.CostEstimate(
            flops=10 * tokens * heads * total_rows * 4 * HEAD, bytes_accessed=4 * 2**20, transcendentals=0
        ),
    )(span_table, queries, out_grad, forward_out, gathered)
    kv_grad = lax.psum_scatter(kv_terms, "ctx", scatter_dimension=0, tiled=True).astype(jnp.bfloat16)
    own = lax.dynamic_slice_in_dim(kv_weight, tp_index * features, features, 0)
    total = dot(kv_grad, own, NT)
    for step in range(1, tp_size):
        other = lax.ppermute(kv_grad, "tp", [(s, (s + step) % tp_size) for s in range(tp_size)])
        total = total + dot(other, weights[step - 1], NT)
    return (query_grad, total.astype(jnp.bfloat16))


def solution(mesh):
    placed = (P("ctx", "tp"), P("ctx", "tp"), P("ctx", "tp"), P("ctx", "tp"), P(None, "tp"), P())
    return jax.shard_map(
        on_device,
        mesh=mesh,
        in_specs=placed,
        out_specs=(P("ctx", "tp"), P("ctx", "tp")),
        check_vma=False,
    )
```

time: 297 us -> 136 us (0.46)
  waiting for transfers between devices: 185 us -> 53.5 us
  Pallas kernels: 0 us -> 31.9 us
  matrix products: 35.3 us -> 4.08 us
  other arithmetic: 25.9 us -> 0.97 us
  local copies, waits for them, and re-layouts: 6.78 us -> 1.26 us
  loops' own time: 4.22 us -> 0 us
  starting transfers between devices: 1.31 us -> 4.95 us
    ppermute x16 -> x3, waiting for transfers between devices: 96.8 us -> 0.09 us  [the longest x1 0.08 us: on_device(): lax.ppermute(kv_grad, 'tp', [(s, (s + step) % tp_size) for s in range(tp_...]
    reduce_scatter x1, waiting for transfers between devices: 87.8 us -> 53.4 us  [on_device(): lax.psum_scatter(kv_terms, 'ctx', scatter_dimension=0, tiled=True)]
    pallas_call x0 -> x1, Pallas kernels: none -> 31.9 us  [on_device(): pl.pallas_call(attention_kernel, out_shape=(jax.ShapeDtypeStruct(queries....]
    dot_general x85 -> x2, matrix products: 35.3 us -> 4.08 us  [dot(): return lax.dot_general(a, b, dims, preferred_element_type=jnp.float32)]
    reduce_sum x26 -> x0, other arithmetic: 19.7 us -> none  [the longest x21 15.7 us: key_positions(): starts = jnp.sum(jnp.where(onehot, span_table[None, :], 0), axis=1)]
    another operation x2 -> x0, loops' own time: 4.22 us -> none  [the longest x1 3.06 us: on_device(): lax.scan(stats_step, (start_top, start_total), block_ids)]
    unnamed x6 -> x0, local copies, waits for them, and re-layouts: 3.96 us -> none
    ppermute x16 -> x3, starting transfers between devices: 1.27 us -> 4.91 us  [the longest x1 3 us: on_device(): lax.ppermute(piece, 'tp', [(s, (s + step) % tp_size) for s in range(tp_si...]
  transfers between devices with their start and end apart: 17 -> 4, of which waited for: 17 -> 2; matrix products, arithmetic and copies ran while one was open for 2% -> 2% of each run, Pallas kernels for 0% -> 24%
where the time goes in v1:
time: 136 us
  waiting for transfers between devices  53.5 us (39%)
  Pallas kernels  31.9 us (23%)
  blocking collectives  24.9 us (18%)
  between operations  14.1 us (10%)
  starting transfers between devices  4.95 us (4%)
  matrix products  4.08 us (3%)
    reduce_scatter x1, waiting for transfers between devices, on_device(): lax.psum_scatter(kv_terms, 'ctx', scatter_dimension=0, tiled=True)  53.4 us
    pallas_call x1, Pallas kernels, on_device(): pl.pallas_call(attention_kernel, out_shape=(jax.ShapeDtypeStruct(queries....  31.9 us
    all_gather x1, blocking collectives, on_device(): gathered = lax.all_gather(keys_values, 'ctx', axis=0, tiled=True)  24.9 us
    dot_general x2, matrix products, dot(): return lax.dot_general(a, b, dims, preferred_element_type=jnp.float32)  4.08 us
    ppermute x1, starting transfers between devices, on_device(): lax.ppermute(piece, 'tp', [(s, (s + step) % tp_size) for s in range(tp_si...  3 us
  transfers between devices with their start and end apart: 4, of which 2 were waited for; matrix products, arithmetic and copies ran while one was open for 2% of the time, Pallas kernels for 24%

profile of v1, /device:TPU:0, one launch (start us, length us, event | category | flops | bytes accessed | tf_op | source)
XLA Modules:
  0.0 135.7 jit_solution(12303983217249602253)
XLA Ops:
  7.2 0.0 reduce-scatter.2.cloned.1.call-start
  7.2 1.3 constant_dynamic-slice_fusion
  8.5 3.0 %collective-permute-start.1 = (bf16[3712,128]{1,0:T(8,128)(2,1)S(1)}, bf16[3712,128]{1,0:T(8,128)(2,1)S(1)}, u32[]{:S(2)}, u32[]{:S(2)}) collective-permute-start(bf16[3712,128]{1,0:T(8,128)(2,1)S(1)} %constant_dynamic-slice_fusion), channel_id=1, source_target_pairs={{0,1},{1,0},{2,3},{3,2},{4,5},{5,4},{6,7},{7,6},{8,9},{9,8},{10,11... | collective-permute-start | bytes 2850824 | tf_op jit(solution)/shard_map/ppermute | solution.py:194
  11.5 24.9 %all_gather.3.kv_ref = bf16[2048,128]{1,0:T(8,128)(2,1)} all-gather(bf16[128,128]{1,0:T(8,128)(2,1)} %param.7), channel_id=1, replica_groups=mesh['ctx'=16,'tp'=2] {'ctx'}, dimensions={0}, use_global_device_ids=true | all-gather | bytes 557056 | tf_op jit(solution)/shard_map/all_gather | solution.py:199
  36.4 31.9 %shard_map.77 = (bf16[128,1024]{1,0:T(8,128)(2,1)}, f32[2048,128]{1,0:T(8,128)}) custom-call(s32[32]{0:T(128)} %table_ref.1, bf16[128,1024]{1,0:T(8,128)(2,1)} %q_ref.1, bf16[128,1024]{1,0:T(8,128)(2,1)} %do_ref.1, bf16[128,1024]{1,0:T(8,128)(2,1)} %fo_ref.1, bf16[2048,128]{1,0:T(8,128)(2,1)} %all_gather.3.kv_ref), custom_call_target="tpu_custom_call" | custom-call | flops 10737418240 | bytes 4194304 | tf_op jit(solution)/shard_map/pallas_call | solution.py:201
  68.3 0.0 reduce-scatter.2.cloned.1.call-update
  68.3 0.0 collective-permute-done.1
  68.3 0.4 collective-permute-start.2
  68.8 53.4 %reduce-scatter.2.cloned.1.call-done = f32[128,128]{1,0:T(8,128)} async-done(((f32[2048,128]{1,0:T(8,128)}), f32[128,128]{1,0:T(8,128)}) %reduce-scatter.2.cloned.1.call-update) | async-done | bytes 65552 | tf_op jit(solution)/shard_map/reduce_scatter | solution.py:215
  122.2 0.8 convert_element_type.6
  123.0 1.5 %collective-permute-start = (bf16[128,128]{1,0:T(8,128)(2,1)S(1)}, bf16[128,128]{1,0:T(8,128)(2,1)S(1)}, u32[]{:S(2)}, u32[]{:S(2)}) collective-permute-start(bf16[128,128]{1,0:T(8,128)(2,1)S(1)} %convert_element_type.6), channel_id=1, source_target_pairs={{0,1},{1,0},{2,3},{3,2},{4,5},{5,4},{6,7},{7,6},{8,9},{9,8},{10,11... | collective-permute-start | bytes 98312 | tf_op jit(solution)/shard_map/ppermute | solution.py:219
  124.5 2.2 %fusion.4 = f32[128,7424]{1,0:T(8,128)S(1)} fusion(bf16[128,128]{1,0:T(8,128)(2,1)S(1)} %convert_element_type.6, bf16[14848,128]{1,0:T(8,128)(2,1)} %param.10, s32[]{:T(128)S(6)} %select_n.29), kind=kOutput, calls=%fused_computation.5 | convolution fusion | flops 243269632 | bytes 5734404 | tf_op jit(solution)/shard_map/dot_general | solution.py:20
  126.7 0.0 collective-permute-done.2
  126.7 0.1 broadcast_select_fusion.1
  126.8 0.1 collective-permute-done
  126.9 1.9 %fusion = bf16[128,7424]{1,0:T(8,128)(2,1)} fusion(f32[128,7424]{1,0:T(8,128)S(1)} %fusion.4, bf16[128,128]{1,0:T(8,128)(2,1)S(1)} %collective-permute-done, bf16[3712,128]{1,0:T(8,128)(2,1)S(1)} %get-tuple-element.7, bf16[3712,128]{1,0:T(8,128)(2,1)S(1)} %get-tuple-element.6), kind=kOutput, calls=%fused_computation.1 | convolution fusion | flops 248971264 | bytes 7634944 | tf_op jit(solution)/shard_map/dot_general | solution.py:20
Async XLA Ops:
  7.2 115.0 %reduce-scatter.2.cloned.1.call-start = ((), (), s32[]{:S(2)}) async-start(), calls=%async_computation.1 | async-start | bytes 1114112 | tf_op jit(solution)/shard_map/reduce_scatter | solution.py:215
  8.5 59.8 %collective-permute-start.1 = (bf16[3712,128]{1,0:T(8,128)(2,1)S(1)}, bf16[3712,128]{1,0:T(8,128)(2,1)S(1)}, u32[]{:S(2)}, u32[]{:S(2)}) collective-permute-start(bf16[3712,128]{1,0:T(8,128)(2,1)S(1)} %constant_dynamic-slice_fusion), channel_id=1, source_target_pairs={{0,1},{1,0},{2,3},{3,2},{4,5},{5,4},{6,7},{7,6},{8,9},{9,8},{10,11... | collective-permute-start | bytes 2850824 | tf_op jit(solution)/shard_map/ppermute | solution.py:194
  68.3 58.3 %collective-permute-start.2 = (bf16[3712,128]{1,0:T(8,128)(2,1)S(1)}, bf16[3712,128]{1,0:T(8,128)(2,1)S(1)}, u32[]{:S(2)}, u32[]{:S(2)}) collective-permute-start(bf16[3712,128]{1,0:T(8,128)(2,1)S(1)} %collective-permute-done.1), channel_id=1, source_target_pairs={{0,2},{2,0},{4,6},{6,4},{8,10},{10,8},{12,14},{14,12},{16,18},{18,... | collective-permute-start | bytes 2850824 | tf_op jit(solution)/shard_map/ppermute | solution.py:195
  123.0 3.9 %collective-permute-start = (bf16[128,128]{1,0:T(8,128)(2,1)S(1)}, bf16[128,128]{1,0:T(8,128)(2,1)S(1)}, u32[]{:S(2)}, u32[]{:S(2)}) collective-permute-start(bf16[128,128]{1,0:T(8,128)(2,1)S(1)} %convert_element_type.6), channel_id=1, source_target_pairs={{0,1},{1,0},{2,3},{3,2},{4,5},{5,4},{6,7},{7,6},{8,9},{9,8},{10,11... | collective-permute-start | bytes 98312 | tf_op jit(solution)/shard_map/ppermute | solution.py:219
Sparse Core Ops, SparseCore 0:
  68.5 53.6 reduce-scatter.1

commit v2 on v1

v2 whole, which is shorter than its diff:
```python
import functools

import jax
import jax.numpy as jnp
from jax import lax
from jax.experimental import pallas as pl
from jax.experimental.pallas import tpu as pltpu
from jax.sharding import PartitionSpec as P

HEAD = 64
CHUNK_HEADS = 8
KEY_TILE = 256
softmax_scale = 0.125
log2_e = 1.4426950408889634
hidden = -1e30

NT = (((1,), (1,)), ((), ()))
NN = (((1,), (0,)), ((), ()))


def dot(a, b, dims=NN):
    return lax.dot_general(a, b, dims, preferred_element_type=jnp.float32)


def spread_queries(table_ref, first_span, half, q_ref, do_ref, fo_ref, qx, qs, dox, dos):
    span_rows = q_ref.shape[0] // 2
    heads = q_ref.shape[1] // HEAD
    span = table_ref[first_span + half]
    row = lax.broadcasted_iota(jnp.int32, (span_rows, 2 * HEAD), 0)
    col = lax.broadcasted_iota(jnp.int32, (span_rows, 2 * HEAD), 1)
    blocked = jnp.where(col < HEAD, col - row, col - HEAD - span) > 0
    mask_cols = jnp.where(blocked, hidden, 0.0).astype(jnp.bfloat16)
    lane = lax.broadcasted_iota(jnp.int32, (span_rows, HEAD), 1)
    rows = pl.ds(half * span_rows, span_rows)
    for head in range(heads):
        pair = pl.ds(head // 2 * 2 * HEAD, 2 * HEAD)
        low = head % 2 * HEAD
        at = pl.ds((half * heads + head) * span_rows, span_rows)
        query = q_ref[rows, pair].astype(jnp.float32)[:, low:low + HEAD]
        grad = do_ref[rows, pair].astype(jnp.float32)[:, low:low + HEAD]
        forward = fo_ref[rows, pair].astype(jnp.float32)[:, low:low + HEAD]
        scaled = query * (softmax_scale * log2_e)
        top = scaled.astype(jnp.bfloat16).astype(jnp.float32)
        qx[at, 0:2 * HEAD] = jnp.concatenate([top, scaled - top], axis=1).astype(jnp.bfloat16)
        qx[at, 2 * HEAD:4 * HEAD] = mask_cols
        blank = jnp.zeros((span_rows, HEAD), jnp.float32)
        qs[at, :] = jnp.concatenate([query * softmax_scale, blank], axis=1).astype(jnp.bfloat16)
        dos[at, :] = jnp.concatenate([blank, grad], axis=1).astype(jnp.bfloat16)
        left = -jnp.sum(grad * forward, axis=1, keepdims=True)
        tail = jnp.zeros((span_rows, HEAD), jnp.float32)
        for place in range(3):
            part = left.astype(jnp.bfloat16).astype(jnp.float32)
            tail = jnp.where(lane == place, part, tail)
            left = left - part
        dox[at, :] = jnp.concatenate([grad, tail], axis=1).astype(jnp.bfloat16)


def spread_keys(table_ref, first_span, first_row, block, kx, kt, vx):
    rows = block.shape[0]
    span_rows = rows // 2
    wide = block.astype(jnp.float32)
    key, value = wide[:, :HEAD], wide[:, HEAD:]
    lane = lax.broadcasted_iota(jnp.int32, (rows, HEAD), 1)
    ones = jnp.where(lane < 3, 1.0, 0.0)
    at = pl.ds(first_row, rows)
    vx[at, :] = jnp.concatenate([value, ones], axis=1).astype(jnp.bfloat16)
    eye = (
        lax.broadcasted_iota(jnp.int32, (HEAD, HEAD), 0)
        == lax.broadcasted_iota(jnp.int32, (HEAD, HEAD), 1)
    ).astype(jnp.bfloat16)
    kt[:, at] = dot(eye, key.astype(jnp.bfloat16), NT).astype(jnp.bfloat16)
    twice = jnp.concatenate([key, key], axis=1).astype(jnp.bfloat16)
    row = lax.broadcasted_iota(jnp.int32, (rows, 2 * HEAD), 0)
    col = lax.broadcasted_iota(jnp.int32, (rows, 2 * HEAD), 1)
    span_index = first_row // span_rows
    span = jnp.where(row < span_rows, table_ref[span_index], table_ref[span_index + 1])
    inner = jnp.where(row < span_rows, row, row - span_rows)
    for half in range(2):
        own = table_ref[first_span + half]
        wanted = jnp.where(col < HEAD, jnp.where(span == own, inner, -1), span + HEAD)
        kx[half, at, 0:2 * HEAD] = twice
        kx[half, at, 2 * HEAD:4 * HEAD] = jnp.where(wanted == col, 1.0, 0.0).astype(jnp.bfloat16)


def attention(chunk_count, chunk_rows, total_rows, span_rows, kx, kt, vx, qx, qs, dox, dos, score, dkv, dq_ref, after_chunk, tile_order, after_tile):
    tiles = total_rows // KEY_TILE
    heads = dq_ref.shape[1] // HEAD

    def chunk_at(chunk):
        return pl.ds(chunk * chunk_rows, chunk_rows)

    def tile_at(tile):
        return pl.ds(pl.multiple_of(tile * KEY_TILE, KEY_TILE), KEY_TILE)

    def score_tile(chunk, tile, top):
        half = chunk * 2 // chunk_count
        s = dot(kx[half, tile_at(tile), :], qx[chunk_at(chunk), :], NT)
        score[chunk % 2, tile_at(tile), :] = s
        return jnp.maximum(top, jnp.max(s.reshape(KEY_TILE // 8, 8, chunk_rows), axis=0))

    def exp_tile(chunk, tile, peak, total):
        e = jnp.exp2(score[chunk % 2, tile_at(tile), :] - peak)
        score[chunk % 2, tile_at(tile), :] = e
        return total + jnp.sum(e.reshape(KEY_TILE // 8, 8, chunk_rows), axis=0)

    top_start = jnp.full((8, chunk_rows), hidden, jnp.float32)
    zero = jnp.zeros((8, chunk_rows), jnp.float32)
    top = lax.fori_loop(0, tiles, lambda tile, top: score_tile(0, tile, top), top_start)
    for chunk in range(chunk_count):
        peak = jnp.max(top, axis=0, keepdims=True)

        def first(tile, running, chunk=chunk, peak=peak):
            top, total = running
            if chunk + 1 < chunk_count:
                top = score_tile(chunk + 1, tile, top)
            return top, exp_tile(chunk, tile, peak, total)

        top, total = lax.fori_loop(0, tiles, first, (top_start, zero))
        inverse = 1.0 / jnp.sum(total, axis=0, keepdims=True)

        def second(tile, dqt, chunk=chunk, inverse=inverse):
            at = tile_at(tile)
            probs = score[chunk % 2, at, :] * inverse
            dprobs = dot(vx[at, :], dox[chunk_at(chunk), :], NT)
            dscores = (probs * dprobs).astype(jnp.bfloat16)
            add = dot(probs.astype(jnp.bfloat16), dos[chunk_at(chunk), :])
            add = add + dot(dscores, qs[chunk_at(chunk), :])
            if chunk == 0:
                dkv[at, :] = add
            else:
                dkv[at, :] += add
            return dqt + dot(kt[:, at], dscores)

        dqt = jnp.zeros((HEAD, chunk_rows), jnp.float32)
        if chunk + 1 < chunk_count:
            dqt = lax.fori_loop(0, tiles, second, dqt)
        else:
            for turn in range(tiles):
                dqt = second(tile_order(turn), dqt)
                after_tile(turn)
        dq = (dqt * softmax_scale).T
        half = chunk * 2 // chunk_count
        first_head = chunk * CHUNK_HEADS % heads
        for pair in range(CHUNK_HEADS // 2):
            parts = [
                dq[(2 * pair + side) * span_rows:(2 * pair + side + 1) * span_rows, :]
                for side in range(2)
            ]
            dq_ref[
                pl.ds(half * span_rows, span_rows),
                pl.ds((first_head + 2 * pair) * HEAD, 2 * HEAD),
            ] = jnp.concatenate(parts, axis=1).astype(jnp.bfloat16)
        after_chunk(chunk)


def weight_pieces(share, most):
    return next(count for count in (4, 2, 1) if count <= most and share % (16 * count) == 0)


def backward_kernel(
    ctx_size, tp_size,
    table_ref, q_ref, do_ref, fo_ref, kv_ref, w_ref,
    dq_ref, grad_ref, wall_ref,
    qx, qs, dox, dos, kx, kt, vx, score, dkv,
    gathered, mate_sum, row_out, row_in, far_out, far_in,
    gz_send, gz_recv, gy_send, gy_recv, gm_send, gm_recv,
    rm_send, rm_recv, ry_send, ry_recv, rz_send, rz_recv,
    wx_send, wx_recv, wm_send, wm_recv, own_sem, t_send, t_recv,
):
    tokens = q_ref.shape[0]
    total_rows = gathered.shape[0]
    far = ctx_size // 4
    me = lax.axis_index("ctx")
    tp = lax.axis_index("tp")
    hi, mid, core = me // 4, lax.rem(me // 2, 2), lax.rem(me, 2)

    def place(h, m, k):
        return h * 4 + m * 2 + k

    def around(step):
        return lax.rem(hi + step, far)

    def behind(step):
        return lax.rem(hi + far - step, far)

    def block(owner):
        return gathered.at[pl.ds(pl.multiple_of(owner * tokens, tokens), tokens), :]

    def send(src, dst, send_sem, recv_sem, axis, target):
        copy = pltpu.make_async_remote_copy(
            src_ref=src, dst_ref=dst, send_sem=send_sem, recv_sem=recv_sem,
            device_id={axis: target}, device_id_type=pl.DeviceIdType.MESH,
        )
        copy.start()
        return copy

    row_mate, core_mate = place(hi, 1 - mid, core), place(hi, mid, 1 - core)
    partners = [("ctx", place(around(step), mid, core)) for step in range(1, far)]
    partners += [("ctx", row_mate), ("ctx", core_mate)]
    partners += [("tp", lax.rem(tp + step, tp_size)) for step in range(1, tp_size)]
    barrier = pltpu.get_barrier_semaphore()
    for axis, target in partners:
        pl.semaphore_signal(barrier, inc=1, device_id={axis: target}, device_id_type=pl.DeviceIdType.MESH)
    pl.semaphore_wait(barrier, len(partners))

    waits = []
    for step in range(1, far):
        waits.append(send(kv_ref, block(me), gz_send.at[step], gz_recv.at[step], "ctx", place(around(step), mid, core)))
    from_far = list(waits)
    from_row = [send(kv_ref, block(me), gy_send.at[0], gy_recv.at[0], "ctx", row_mate)]
    from_core = [send(kv_ref, block(me), gm_send.at[0, 0], gm_recv.at[0, 0], "ctx", core_mate)]

    features = w_ref.shape[0] // tp_size
    share = features // 2
    pieces = weight_pieces(share, wx_send.shape[1])
    piece_rows = share // pieces
    own_copy = pltpu.make_async_copy(
        w_ref.at[pl.ds(pl.multiple_of(tp * features, 16), features), :], wall_ref.at[:, pl.ds(0, 2 * HEAD)], own_sem
    )
    own_copy.start()

    def wall_piece(step, side, piece):
        first = pl.multiple_of(side * share + piece * piece_rows, 16)
        return wall_ref.at[pl.ds(first, piece_rows), pl.ds(step * 2 * HEAD, 2 * HEAD)]

    weight_in = {}
    for piece in range(pieces):
        for step in range(1, tp_size):
            target = lax.rem(tp + step, tp_size)
            first = pl.multiple_of(target * features + core * share + piece * piece_rows, 16)
            weight_in[step, piece] = send(
                w_ref.at[pl.ds(first, piece_rows), :], wall_piece(step, core, piece),
                wx_send.at[step, piece], wx_recv.at[step, piece], "tp", target,
            )
    weight_mate = []

    first_span = me * 2
    spread_queries(table_ref, first_span, 0, q_ref, do_ref, fo_ref, qx, qs, dox, dos)
    for step in range(1, far):
        from_far[step - 1].wait_recv()
        here = block(place(behind(step), mid, core))
        from_row.append(send(here, here, gy_send.at[step], gy_recv.at[step], "ctx", row_mate))
        from_core.append(send(here, here, gm_send.at[step, 0], gm_recv.at[step, 0], "ctx", core_mate))
    spread_queries(table_ref, first_span, 1, q_ref, do_ref, fo_ref, qx, qs, dox, dos)
    for step in range(far):
        from_row[step].wait_recv()
        here = block(place(behind(step), 1 - mid, core))
        from_core.append(send(here, here, gm_send.at[step, 1], gm_recv.at[step, 1], "ctx", core_mate))

    def take(owner, ref):
        first_row = pl.multiple_of(owner * tokens, tokens)
        spread_keys(table_ref, first_span, first_row, ref[...], kx, kt, vx)

    take(me, kv_ref)

    @pl.loop(1, 2 * far)
    def _(turn):
        owner = place(behind(turn // 2), lax.rem(mid + lax.rem(turn, 2), 2), core)
        take(owner, block(owner))

    for copy in from_core:
        copy.wait_recv()

    @pl.loop(0, 2 * far)
    def _(turn):
        owner = place(behind(turn // 2), lax.rem(mid + lax.rem(turn, 2), 2), 1 - core)
        take(owner, block(owner))

    for copy in from_far + from_row + from_core:
        copy.wait_send()

    def after_chunk(chunk):
        if chunk < pieces:
            for step in range(1, tp_size):
                weight_in[step, chunk].wait_recv()
                here = wall_piece(step, core, chunk)
                weight_mate.append(
                    send(here, here, wm_send.at[step, chunk], wm_recv.at[step, chunk], "ctx", core_mate)
                )

    def turn_place(turn):
        return around(turn % far + 1), (1 - mid if turn < far else mid)

    def tile_order(turn):
        h, m = turn_place(turn)
        return h * 2 + m

    def part(turn, k):
        h, m = turn_place(turn)
        return pl.ds(pl.multiple_of(place(h, m, k) * tokens, tokens), tokens)

    to_core, to_row, to_far = [], [], []

    def pass_on(turn):
        to_core[turn].wait_recv()
        total = dkv[part(turn, core), :] + mate_sum[turn]
        step = turn % far
        if turn < far:
            row_out[step] = total.astype(jnp.bfloat16)
            to_row.append(send(row_out.at[step], row_in.at[step], ry_send.at[step], ry_recv.at[step], "ctx", row_mate))
            return
        to_row[step].wait_recv()
        total = total + row_in[step].astype(jnp.float32)
        if step + 1 < far:
            far_out[step] = total.astype(jnp.bfloat16)
            h, _ = turn_place(turn)
            to_far.append(
                send(far_out.at[step], far_in.at[step], rz_send.at[step], rz_recv.at[step], "ctx", place(h, mid, core))
            )
            return
        for copy in to_far:
            copy.wait_recv()
        for step in range(far - 1):
            total = total + far_in[step].astype(jnp.float32)
        grad_ref[:, 0:2 * HEAD] = total.astype(jnp.bfloat16)

    lag = 2

    def after_tile(turn):
        to_core.append(
            send(dkv.at[part(turn, 1 - core), :], mate_sum.at[turn], rm_send.at[turn], rm_recv.at[turn], "ctx", core_mate)
        )
        if turn >= lag:
            pass_on(turn - lag)

    chunk_rows = CHUNK_HEADS * tokens // 2
    chunk_count = qx.shape[0] // chunk_rows
    attention(
        chunk_count, chunk_rows, total_rows, tokens // 2, kx, kt, vx, qx, qs, dox, dos, score, dkv, dq_ref,
        after_chunk, tile_order, after_tile,
    )
    for turn in range(2 * far - lag, 2 * far):
        pass_on(turn)
    last = []
    for step in range(1, tp_size):
        last.append(
            send(
                grad_ref.at[:, pl.ds(0, 2 * HEAD)], grad_ref.at[:, pl.ds(step * 2 * HEAD, 2 * HEAD)],
                t_send.at[step], t_recv.at[step], "tp", lax.rem(tp + step, tp_size),
            )
        )
    for copy in to_core + to_row + to_far + list(weight_in.values()):
        copy.wait_send()
    for copy in weight_mate + last:
        copy.wait()
    own_copy.wait()


def scratch(tokens, heads, ctx_size, tp_size):
    total_rows = tokens * ctx_size
    rows = tokens * heads
    chunk_rows = CHUNK_HEADS * tokens // 2
    far = ctx_size // 4
    block = (tokens, 2 * HEAD)
    sems = pltpu.SemaphoreType.DMA
    return [
        pltpu.VMEM((rows, 4 * HEAD), jnp.bfloat16),
        pltpu.VMEM((rows, 2 * HEAD), jnp.bfloat16),
        pltpu.VMEM((rows, 2 * HEAD), jnp.bfloat16),
        pltpu.VMEM((rows, 2 * HEAD), jnp.bfloat16),
        pltpu.VMEM((2, total_rows, 4 * HEAD), jnp.bfloat16),
        pltpu.VMEM((HEAD, total_rows), jnp.bfloat16),
        pltpu.VMEM((total_rows, 2 * HEAD), jnp.bfloat16),
        pltpu.VMEM((2, total_rows, chunk_rows), jnp.float32),
        pltpu.VMEM((total_rows, 2 * HEAD), jnp.float32),
        pltpu.VMEM((total_rows, 2 * HEAD), jnp.bfloat16),
        pltpu.VMEM((2 * far,) + block, jnp.float32),
        pltpu.VMEM((far,) + block, jnp.bfloat16),
        pltpu.VMEM((far,) + block, jnp.bfloat16),
        pltpu.VMEM((far,) + block, jnp.bfloat16),
        pltpu.VMEM((far,) + block, jnp.bfloat16),
        sems((far,)), sems((far,)), sems((far,)), sems((far,)), sems((far, 2)), sems((far, 2)),
        sems((2 * far,)), sems((2 * far,)), sems((far,)), sems((far,)), sems((far,)), sems((far,)),
        sems((tp_size, 4)), sems((tp_size, 4)), sems((tp_size, 4)), sems((tp_size, 4)), sems(()),
        sems((tp_size,)), sems((tp_size,)),
    ]


def on_device(queries, keys_values, forward_out, out_grad, kv_weight, span_table):
    tokens = queries.shape[0]
    heads = queries.shape[1] // HEAD
    tp_size = lax.axis_size("tp")
    ctx_size = lax.axis_size("ctx")
    features = kv_weight.shape[0] // tp_size
    vmem = pl.BlockSpec(memory_space=pltpu.VMEM)
    anywhere = pl.BlockSpec(memory_space=pl.ANY)
    query_grad, kv_grad, weights = pl.pallas_call(
        functools.partial(backward_kernel, ctx_size, tp_size),
        out_shape=(
            jax.ShapeDtypeStruct(queries.shape, jnp.bfloat16),
            jax.ShapeDtypeStruct((tokens, tp_size * 2 * HEAD), jnp.bfloat16),
            jax.ShapeDtypeStruct((features, tp_size * 2 * HEAD), jnp.bfloat16),
        ),
        in_specs=[pl.BlockSpec(memory_space=pltpu.SMEM)] + [vmem] * 4 + [anywhere],
        out_specs=(vmem, vmem, anywhere),
        scratch_shapes=scratch(tokens, heads, ctx_size, tp_size),
        compiler_params=pltpu.CompilerParams(
            vmem_limit_bytes=56 * 2**20, collective_id=0, has_side_effects=True
        ),
    )(span_table, queries, out_grad, forward_out, keys_values, kv_weight)
    return (query_grad, dot(kv_grad, weights, NT).astype(jnp.bfloat16))


def solution(mesh):
    placed = (P("ctx", "tp"), P("ctx", "tp"), P("ctx", "tp"), P("ctx", "tp"), P(None, "tp"), P())
    return jax.shard_map(
        on_device,
        mesh=mesh,
        in_specs=placed,
        out_specs=(P("ctx", "tp"), P("ctx", "tp")),
        check_vma=False,
    )
```

time: 136 us -> 72.8 us (0.54)
  waiting for transfers between devices: 53.5 us -> 0 us
  Pallas kernels: 31.9 us -> 66.5 us
  blocking collectives: 24.9 us -> 0 us
  between operations: 14.1 us -> 0.65 us
  starting transfers between devices: 4.95 us -> 0 us
    reduce_scatter x1 -> x0, waiting for transfers between devices: 53.4 us -> none  [on_device(): lax.psum_scatter(kv_terms, 'ctx', scatter_dimension=0, tiled=True)]
    pallas_call x1, Pallas kernels: 31.9 us -> 66.5 us  [on_device(): pl.pallas_call(functools.partial(backward_kernel, ctx_size, tp_size), out...]
    all_gather x1 -> x0, blocking collectives: 24.9 us -> none  [on_device(): gathered = lax.all_gather(keys_values, 'ctx', axis=0, tiled=True)]
    ppermute x3 -> x0, starting transfers between devices: 4.91 us -> none  [the longest x1 3 us: on_device(): lax.ppermute(piece, 'tp', [(s, (s + step) % tp_size) for s in range(tp_si...]
    dot_general x2 -> x1, matrix products: 4.08 us -> 4.8 us  [dot(): return lax.dot_general(a, b, dims, preferred_element_type=jnp.float32)]
  transfers between devices with their start and end apart: 4 -> 0, of which waited for: 2 -> 0; matrix products, arithmetic and copies ran while one was open for 2% -> 0% of each run, Pallas kernels for 24% -> 0%
where the time goes in v2:
time: 72.8 us; the launch traced here: 72.7 us
  Pallas kernels  66.5 us (91%)
  matrix products  4.8 us (7%)
    pallas_call x1, Pallas kernels, on_device(): pl.pallas_call(functools.partial(backward_kernel, ctx_size, tp_size), out...  66.5 us
    dot_general x1, matrix products, dot(): return lax.dot_general(a, b, dims, preferred_element_type=jnp.float32)  4.8 us

profile of v2, /device:TPU:0, one launch (start us, length us, event | category | flops | bytes accessed | tf_op | source)
XLA Modules:
  0.0 72.7 jit_solution(6013223308416105310)
XLA Ops:
  0.6 66.5 %shard_map.77 = (bf16[128,1024]{1,0:T(8,128)(2,1)}, bf16[128,256]{1,0:T(8,128)(2,1)}, bf16[7424,256]{1,0:T(8,128)(2,1)}) custom-call(s32[32]{0:T(128)} %table_ref.1, bf16[128,1024]{1,0:T(8,128)(2,1)} %q_ref.1, bf16[128,1024]{1,0:T(8,128)(2,1)} %do_ref.1, bf16[128,1024]{1,0:T(8,128)(2,1)} %fo_ref.1, bf16[128,128]{1,0:T(8,128)(2,1)} %kv_ref.1, ...), custom_call_target="tpu_custom_call" | custom-call | tf_op jit(solution)/shard_map/pallas_call | solution.py:387
  67.2 0.0 copy-start
  67.2 4.8 %convolution_convert_fusion = bf16[128,7424]{1,0:T(8,128)(2,1)} fusion(bf16[128,256]{1,0:T(8,128)(2,1)} %get-tuple-element.6, bf16[7424,256]{1,0:T(8,128)(2,1)} %get-tuple-element.7), kind=kOutput, calls=%fused_computation | convolution fusion | flops 487489536 | bytes 5767168 | tf_op jit(solution)/shard_map/dot_general | solution.py:22
  72.0 0.0 copy-done
  72.0 0.7 copy.9
Async XLA Ops:
  67.2 4.8 %copy-start = (bf16[128,1024]{1,0:T(8,128)(2,1)S(1)}, bf16[128,1024]{1,0:T(8,128)(2,1)}, u32[]{:S(2)}) copy-start(bf16[128,1024]{1,0:T(8,128)(2,1)} %get-tuple-element.10) | copy-start | bytes 786436

commit v3 on v2

--- a/solution.py
+++ b/solution.py
@@ -90,7 +90,10 @@
         return pl.ds(chunk * chunk_rows, chunk_rows)
 
     def tile_at(tile):
-        return pl.ds(pl.multiple_of(tile * KEY_TILE, KEY_TILE), KEY_TILE)
+        first_row = tile * KEY_TILE
+        if not isinstance(tile, int):
+            first_row = pl.multiple_of(first_row, KEY_TILE)
+        return pl.ds(first_row, KEY_TILE)
 
     def score_tile(chunk, tile, top):
         half = chunk * 2 // chunk_count
@@ -105,17 +108,17 @@
 
     top_start = jnp.full((8, chunk_rows), hidden, jnp.float32)
     zero = jnp.zeros((8, chunk_rows), jnp.float32)
-    top = lax.fori_loop(0, tiles, lambda tile, top: score_tile(0, tile, top), top_start)
+    top = top_start
+    for tile in range(tiles):
+        top = score_tile(0, tile, top)
     for chunk in range(chunk_count):
         peak = jnp.max(top, axis=0, keepdims=True)
 
-        def first(tile, running, chunk=chunk, peak=peak):
-            top, total = running
+        top, total = top_start, zero
+        for tile in range(tiles):
             if chunk + 1 < chunk_count:
                 top = score_tile(chunk + 1, tile, top)
-            return top, exp_tile(chunk, tile, peak, total)
-
-        top, total = lax.fori_loop(0, tiles, first, (top_start, zero))
+            total = exp_tile(chunk, tile, peak, total)
         inverse = 1.0 / jnp.sum(total, axis=0, keepdims=True)
 
         def second(tile, dqt, chunk=chunk, inverse=inverse):
@@ -132,10 +135,10 @@
             return dqt + dot(kt[:, at], dscores)
 
         dqt = jnp.zeros((HEAD, chunk_rows), jnp.float32)
-        if chunk + 1 < chunk_count:
-            dqt = lax.fori_loop(0, tiles, second, dqt)
-        else:
-            for turn in range(tiles):
+        for turn in range(tiles):
+            if chunk + 1 < chunk_count:
+                dqt = second(turn, dqt)
+            else:
                 dqt = second(tile_order(turn), dqt)
                 after_tile(turn)
         dq = (dqt * softmax_scale).T
@@ -215,13 +218,13 @@
     pieces = weight_pieces(share, wx_send.shape[1])
     piece_rows = share // pieces
     own_copy = pltpu.make_async_copy(
-        w_ref.at[pl.ds(pl.multiple_of(tp * features, 16), features), :], wall_ref.at[:, pl.ds(0, 2 * HEAD)], own_sem
+        w_ref.at[pl.ds(pl.multiple_of(tp * features, 16), features), :], wall_ref.at[0], own_sem
     )
     own_copy.start()
 
     def wall_piece(step, side, piece):
         first = pl.multiple_of(side * share + piece * piece_rows, 16)
-        return wall_ref.at[pl.ds(first, piece_rows), pl.ds(step * 2 * HEAD, 2 * HEAD)]
+        return wall_ref.at[step, pl.ds(first, piece_rows), :]
 
     weight_in = {}
     for piece in range(pieces):
@@ -269,14 +272,17 @@
     for copy in from_far + from_row + from_core:
         copy.wait_send()
 
+    def share_weights(piece):
+        for step in range(1, tp_size):
+            weight_in[step, piece].wait_recv()
+            here = wall_piece(step, core, piece)
+            weight_mate.append(
+                send(here, here, wm_send.at[step, piece], wm_recv.at[step, piece], "ctx", core_mate)
+            )
+
     def after_chunk(chunk):
-        if chunk < pieces:
-            for step in range(1, tp_size):
-                weight_in[step, chunk].wait_recv()
-                here = wall_piece(step, core, chunk)
-                weight_mate.append(
-                    send(here, here, wm_send.at[step, chunk], wm_recv.at[step, chunk], "ctx", core_mate)
-                )
+        if 1 <= chunk <= pieces:
+            share_weights(chunk - 1)
 
     def turn_place(turn):
         return around(turn % far + 1), (1 - mid if turn < far else mid)
@@ -312,9 +318,9 @@
             copy.wait_recv()
         for step in range(far - 1):
             total = total + far_in[step].astype(jnp.float32)
-        grad_ref[:, 0:2 * HEAD] = total.astype(jnp.bfloat16)
-
-    lag = 2
+        grad_ref[0] = total.astype(jnp.bfloat16)
+
+    lag = 3
 
     def after_tile(turn):
         to_core.append(
@@ -331,11 +337,13 @@
     )
     for turn in range(2 * far - lag, 2 * far):
         pass_on(turn)
+    for piece in range(chunk_count - 1, pieces):
+        share_weights(piece)
     last = []
     for step in range(1, tp_size):
         last.append(
             send(
-                grad_ref.at[:, pl.ds(0, 2 * HEAD)], grad_ref.at[:, pl.ds(step * 2 * HEAD, 2 * HEAD)],
+                grad_ref.at[0], grad_ref.at[step],
                 t_send.at[step], t_recv.at[step], "tp", lax.rem(tp + step, tp_size),
             )
         )
@@ -344,6 +352,43 @@
     for copy in weight_mate + last:
         copy.wait()
     own_copy.wait()
+
+
+def feature_chunks(features):
+    if features % 128:
+        return [(0, features)]
+    step = 1024
+    return [(first, min(step, features - first)) for first in range(0, features, step)]
+
+
+def project_kernel(chunks, grad_ref, w_ref, out_ref, w_buf, out_buf, in_sem, out_sem):
+    tp_size = w_ref.shape[0]
+    arrivals = []
+    for index, (first, count) in enumerate(chunks):
+        arrivals.append([
+            pltpu.make_async_copy(
+                w_ref.at[step, pl.ds(first, count), :],
+                w_buf.at[pl.ds(first, count), pl.ds(step * 2 * HEAD, 2 * HEAD)],
+                in_sem.at[index, step],
+            )
+            for step in range(tp_size)
+        ])
+        for copy in arrivals[-1]:
+            copy.start()
+    grad = jnp.concatenate([grad_ref[step] for step in range(tp_size)], axis=1)
+    leaving = []
+    for index, (first, count) in enumerate(chunks):
+        for copy in arrivals[index]:
+            copy.wait()
+        out_buf[:, first:first + count] = dot(grad, w_buf[first:first + count, :], NT).astype(jnp.bfloat16)
+        leaving.append(
+            pltpu.make_async_copy(
+                out_buf.at[:, pl.ds(first, count)], out_ref.at[:, pl.ds(first, count)], out_sem.at[index]
+            )
+        )
+        leaving[-1].start()
+    for copy in leaving:
+        copy.wait()
 
 
 def scratch(tokens, heads, ctx_size, tp_size):
@@ -388,8 +433,8 @@
         functools.partial(backward_kernel, ctx_size, tp_size),
         out_shape=(
             jax.ShapeDtypeStruct(queries.shape, jnp.bfloat16),
-            jax.ShapeDtypeStruct((tokens, tp_size * 2 * HEAD), jnp.bfloat16),
-            jax.ShapeDtypeStruct((features, tp_size * 2 * HEAD), jnp.bfloat16),
+            jax.ShapeDtypeStruct((tp_size, tokens, 2 * HEAD), jnp.bfloat16),
+            jax.ShapeDtypeStruct((tp_size, features, 2 * HEAD), jnp.bfloat16),
         ),
         in_specs=[pl.BlockSpec(memory_space=pltpu.SMEM)] + [vmem] * 4 + [anywhere],
         out_specs=(vmem, vmem, anywhere),
@@ -398,7 +443,21 @@
             vmem_limit_bytes=56 * 2**20, collective_id=0, has_side_effects=True
         ),
     )(span_table, queries, out_grad, forward_out, keys_values, kv_weight)
-    return (query_grad, dot(kv_grad, weights, NT).astype(jnp.bfloat16))
+    chunks = feature_chunks(features)
+    input_grad = pl.pallas_call(
+        functools.partial(project_kernel, chunks),
+        out_shape=jax.ShapeDtypeStruct((tokens, features), jnp.bfloat16),
+        in_specs=[vmem, anywhere],
+        out_specs=anywhere,
+        scratch_shapes=[
+            pltpu.VMEM((features, tp_size * 2 * HEAD), jnp.bfloat16),
+            pltpu.VMEM((tokens, features), jnp.bfloat16),
+            pltpu.SemaphoreType.DMA((len(chunks), tp_size)),
+            pltpu.SemaphoreType.DMA((len(chunks),)),
+        ],
+        compiler_params=pltpu.CompilerParams(vmem_limit_bytes=24 * 2**20),
+    )(kv_grad, weights)
+    return (query_grad, input_grad)
 
 
 def solution(mesh):

time: 72.8 us -> 74.9 us (1.029)
  matrix products: 4.8 us -> 0 us
  Pallas kernels: 66.5 us -> 70.4 us
  local copies, waits for them, and re-layouts: 0.71 us -> 3.62 us
    dot_general x1 -> x0, matrix products: 4.8 us -> none  [dot(): return lax.dot_general(a, b, dims, preferred_element_type=jnp.float32)]
    pallas_call x0 -> x1, Pallas kernels: none -> 3.89 us  [on_device(): pl.pallas_call(functools.partial(project_kernel, chunks), out_shape=jax.S...]
    unnamed x3 -> x7, local copies, waits for them, and re-layouts: 0.71 us -> 3.62 us
where the time goes in v3:
time: 74.9 us; the launch traced here: 74.7 us
  Pallas kernels  70.4 us (94%)
  local copies, waits for them, and re-layouts  3.62 us (5%)
    pallas_call x1, Pallas kernels, on_device(): pl.pallas_call(functools.partial(backward_kernel, ctx_size, tp_size), out...  66.5 us
    pallas_call x1, Pallas kernels, on_device(): pl.pallas_call(functools.partial(project_kernel, chunks), out_shape=jax.S...  3.89 us
    unnamed x7, local copies, waits for them, and re-layouts  3.62 us

profile of v3, /device:TPU:0, one launch (start us, length us, event | category | flops | bytes accessed | tf_op | source)
XLA Modules:
  0.0 74.7 jit_solution(1261466451207432624)
XLA Ops:
  0.6 66.5 %shard_map.77 = (bf16[128,1024]{1,0:T(8,128)(2,1)}, bf16[2,128,128]{2,1,0:T(8,128)(2,1)}, bf16[2,7424,128]{2,1,0:T(8,128)(2,1)}) custom-call(s32[32]{0:T(128)} %table_ref.1, bf16[128,1024]{1,0:T(8,128)(2,1)} %q_ref.1, bf16[128,1024]{1,0:T(8,128)(2,1)} %do_ref.1, bf16[128,1024]{1,0:T(8,128)(2,1)} %fo_ref.1, bf16[128,128]{1,0:T(8,128)(2,1)} %kv_ref.1, ...), custom_call_target="tpu_custom_call" | custom-call | tf_op jit(solution)/shard_map/pallas_call | solution.py:432
  67.2 0.0 copy-start
  67.2 2.1 %copy-done = bf16[2,7424,128]{2,1,0:T(8,128)(2,1)S(1)} copy-done((bf16[2,7424,128]{2,1,0:T(8,128)(2,1)S(1)}, bf16[2,7424,128]{2,1,0:T(8,128)(2,1)}, u32[]{:S(2)}) %copy-start) | copy-done | bytes 3801112
  69.3 0.0 copy-start.1
  69.3 0.8 %copy-done.1 = bf16[2,128,128]{2,1,0:T(8,128)(2,1)S(1)} copy-done((bf16[2,128,128]{2,1,0:T(8,128)(2,1)S(1)}, bf16[2,128,128]{2,1,0:T(8,128)(2,1)}, u32[]{:S(2)}) %copy-start.1) | copy-done | bytes 65560
  70.1 0.0 copy-start.2
  70.1 3.9 %shard_map.78 = bf16[128,7424]{1,0:T(8,128)(2,1)} custom-call(bf16[2,128,128]{2,1,0:T(8,128)(2,1)S(1)} %copy-done.1, bf16[2,7424,128]{2,1,0:T(8,128)(2,1)S(1)} %copy-done), custom_call_target="tpu_custom_call" | custom-call | tf_op jit(solution)/shard_map/pallas_call | solution.py:447
  74.0 0.0 copy-done.2
  74.0 0.7 copy.9
Async XLA Ops:
  67.2 2.1 %copy-start = (bf16[2,7424,128]{2,1,0:T(8,128)(2,1)S(1)}, bf16[2,7424,128]{2,1,0:T(8,128)(2,1)}, u32[]{:S(2)}) copy-start(bf16[2,7424,128]{2,1,0:T(8,128)(2,1)} %get-tuple-element.7.w_ref) | copy-start | bytes 11403268
  69.3 0.8 %copy-start.1 = (bf16[2,128,128]{2,1,0:T(8,128)(2,1)S(1)}, bf16[2,128,128]{2,1,0:T(8,128)(2,1)}, u32[]{:S(2)}) copy-start(bf16[2,128,128]{2,1,0:T(8,128)(2,1)} %get-tuple-element.6.grad_ref) | copy-start | bytes 196612
  70.1 3.9 %copy-start.2 = (bf16[128,1024]{1,0:T(8,128)(2,1)S(1)}, bf16[128,1024]{1,0:T(8,128)(2,1)}, u32[]{:S(2)}) copy-start(bf16[128,1024]{1,0:T(8,128)(2,1)} %get-tuple-element.10) | copy-start | bytes 786436

commit v4 on v3

--- a/solution.py
+++ b/solution.py
@@ -163,12 +163,13 @@
 def backward_kernel(
     ctx_size, tp_size,
     table_ref, q_ref, do_ref, fo_ref, kv_ref, w_ref,
-    dq_ref, grad_ref, wall_ref,
+    dq_ref, out_ref,
     qx, qs, dox, dos, kx, kt, vx, score, dkv,
-    gathered, mate_sum, row_out, row_in, far_out, far_in,
+    gathered, mate_sum, row_out, row_in, far_out, far_in, grad_ref, wall_ref, staged, out_buf,
     gz_send, gz_recv, gy_send, gy_recv, gm_send, gm_recv,
     rm_send, rm_recv, ry_send, ry_recv, rz_send, rz_recv,
     wx_send, wx_recv, wm_send, wm_recv, own_sem, t_send, t_recv,
+    stage_sem, bx_send, bx_recv, bz_send, bz_recv, by_send, by_recv, bm_send, bm_recv, out_sem,
 ):
     tokens = q_ref.shape[0]
     total_rows = gathered.shape[0]
@@ -201,6 +202,29 @@
     partners = [("ctx", place(around(step), mid, core)) for step in range(1, far)]
     partners += [("ctx", row_mate), ("ctx", core_mate)]
     partners += [("tp", lax.rem(tp + step, tp_size)) for step in range(1, tp_size)]
+    features = w_ref.shape[0] // tp_size
+    spread = spread_block(features, ctx_size)
+    spread_rows = spread * ctx_size
+    share = (features - spread_rows) // 2
+    pieces = weight_pieces(share, wx_send.shape[1])
+    piece_rows = share // pieces
+    own_copy = pltpu.make_async_copy(
+        w_ref.at[pl.ds(pl.multiple_of(tp * features, 16), features), :], wall_ref.at[0], own_sem
+    )
+    staging = []
+    for step in range(1, tp_size):
+        target = lax.rem(tp + step, tp_size) * features
+        first = pl.multiple_of(target + me * spread, 16)
+        staging.append(pltpu.make_async_copy(
+            w_ref.at[pl.ds(first, spread), :], staged.at[step - 1, pl.ds(0, spread), :], stage_sem.at[step, 0]
+        ))
+        first = pl.multiple_of(target + spread_rows + core * share, 16)
+        staging.append(pltpu.make_async_copy(
+            w_ref.at[pl.ds(first, share), :], staged.at[step - 1, pl.ds(spread, share), :], stage_sem.at[step, 1]
+        ))
+    for copy in staging:
+        copy.start()
+
     barrier = pltpu.get_barrier_semaphore()
     for axis, target in partners:
         pl.semaphore_signal(barrier, inc=1, device_id={axis: target}, device_id_type=pl.DeviceIdType.MESH)
@@ -213,29 +237,61 @@
     from_row = [send(kv_ref, block(me), gy_send.at[0], gy_recv.at[0], "ctx", row_mate)]
     from_core = [send(kv_ref, block(me), gm_send.at[0, 0], gm_recv.at[0, 0], "ctx", core_mate)]
 
-    features = w_ref.shape[0] // tp_size
-    share = features // 2
-    pieces = weight_pieces(share, wx_send.shape[1])
-    piece_rows = share // pieces
-    own_copy = pltpu.make_async_copy(
-        w_ref.at[pl.ds(pl.multiple_of(tp * features, 16), features), :], wall_ref.at[0], own_sem
-    )
     own_copy.start()
+    for copy in staging:
+        copy.wait()
 
     def wall_piece(step, side, piece):
-        first = pl.multiple_of(side * share + piece * piece_rows, 16)
+        first = pl.multiple_of(spread_rows + side * share + piece * piece_rows, 16)
         return wall_ref.at[step, pl.ds(first, piece_rows), :]
 
+    def wall_block(step, owner):
+        return wall_ref.at[step, pl.ds(pl.multiple_of(owner * spread, 16), spread), :]
+
+    block_in = {}
+    for step in range(1, tp_size):
+        block_in[step] = send(
+            staged.at[step - 1, pl.ds(0, spread), :], wall_block(step, me),
+            bx_send.at[step], bx_recv.at[step], "tp", lax.rem(tp + step, tp_size),
+        )
     weight_in = {}
     for piece in range(pieces):
         for step in range(1, tp_size):
-            target = lax.rem(tp + step, tp_size)
-            first = pl.multiple_of(target * features + core * share + piece * piece_rows, 16)
             weight_in[step, piece] = send(
-                w_ref.at[pl.ds(first, piece_rows), :], wall_piece(step, core, piece),
-                wx_send.at[step, piece], wx_recv.at[step, piece], "tp", target,
+                staged.at[step - 1, pl.ds(spread + piece * piece_rows, piece_rows), :], wall_piece(step, core, piece),
+                wx_send.at[step, piece], wx_recv.at[step, piece], "tp", lax.rem(tp + step, tp_size),
             )
-    weight_mate = []
+    weight_mate, block_far, block_row, block_core = [], {}, {}, []
+
+    def block_to_mates(step, hop):
+        here = wall_block(step, place(behind(hop), mid, core))
+        block_row[step, hop] = send(here, here, by_send.at[step, hop], by_recv.at[step, hop], "ctx", row_mate)
+        block_core.append(send(here, here, bm_send.at[step, hop, 0], bm_recv.at[step, hop, 0], "ctx", core_mate))
+
+    def spread_own_blocks():
+        for step in range(1, tp_size):
+            block_in[step].wait_recv()
+            here = wall_block(step, me)
+            for hop in range(1, far):
+                block_far[step, hop] = send(
+                    here, here, bz_send.at[step, hop], bz_recv.at[step, hop], "ctx", place(around(hop), mid, core)
+                )
+            block_to_mates(step, 0)
+
+    def spread_far_blocks():
+        for step in range(1, tp_size):
+            for hop in range(1, far):
+                block_far[step, hop].wait_recv()
+                block_to_mates(step, hop)
+
+    def spread_row_blocks():
+        for step in range(1, tp_size):
+            for hop in range(far):
+                block_row[step, hop].wait_recv()
+                here = wall_block(step, place(behind(hop), 1 - mid, core))
+                block_core.append(
+                    send(here, here, bm_send.at[step, hop, 1], bm_recv.at[step, hop, 1], "ctx", core_mate)
+                )
 
     first_span = me * 2
     spread_queries(table_ref, first_span, 0, q_ref, do_ref, fo_ref, qx, qs, dox, dos)
@@ -280,9 +336,15 @@
                 send(here, here, wm_send.at[step, piece], wm_recv.at[step, piece], "ctx", core_mate)
             )
 
+    spread_own_blocks()
+
     def after_chunk(chunk):
-        if 1 <= chunk <= pieces:
-            share_weights(chunk - 1)
+        if chunk == 0:
+            spread_far_blocks()
+        if chunk == 1:
+            spread_row_blocks()
+        if chunk + 1 < chunk_count and chunk < pieces:
+            share_weights(chunk)
 
     def turn_place(turn):
         return around(turn % far + 1), (1 - mid if turn < far else mid)
@@ -336,9 +398,10 @@
         after_chunk, tile_order, after_tile,
     )
     for turn in range(2 * far - lag, 2 * far):
+        if turn + 1 == 2 * far:
+            for piece in range(chunk_count - 1, pieces):
+                share_weights(piece)
         pass_on(turn)
-    for piece in range(chunk_count - 1, pieces):
-        share_weights(piece)
     last = []
     for step in range(1, tp_size):
         last.append(
@@ -347,11 +410,28 @@
                 t_send.at[step], t_recv.at[step], "tp", lax.rem(tp + step, tp_size),
             )
         )
-    for copy in to_core + to_row + to_far + list(weight_in.values()):
+    for copy in last + weight_mate + block_core:
+        copy.wait_recv()
+    own_copy.wait()
+    grad = jnp.concatenate([grad_ref[step] for step in range(tp_size)], axis=1)
+    leaving = []
+    for index, (first, count) in enumerate(feature_chunks(features)):
+        at = pl.ds(first, count)
+        weights = jnp.concatenate([wall_ref[step, at, :] for step in range(tp_size)], axis=1)
+        out_buf[:, at] = dot(grad, weights, NT).astype(jnp.bfloat16)
+        leaving.append(pltpu.make_async_copy(out_buf.at[:, at], out_ref.at[:, at], out_sem.at[index]))
+        leaving[-1].start()
+    for copy in to_core + to_row + to_far + last + weight_mate + block_core:
         copy.wait_send()
-    for copy in weight_mate + last:
+    for copies in (weight_in, block_in, block_far, block_row):
+        for copy in copies.values():
+            copy.wait_send()
+    for copy in leaving:
         copy.wait()
-    own_copy.wait()
+
+
+def spread_block(features, ctx_size):
+    return 16 * (features * 11 // (20 * 16 * ctx_size))
 
 
 def feature_chunks(features):
@@ -361,42 +441,14 @@
     return [(first, min(step, features - first)) for first in range(0, features, step)]
 
 
-def project_kernel(chunks, grad_ref, w_ref, out_ref, w_buf, out_buf, in_sem, out_sem):
-    tp_size = w_ref.shape[0]
-    arrivals = []
-    for index, (first, count) in enumerate(chunks):
-        arrivals.append([
-            pltpu.make_async_copy(
-                w_ref.at[step, pl.ds(first, count), :],
-                w_buf.at[pl.ds(first, count), pl.ds(step * 2 * HEAD, 2 * HEAD)],
-                in_sem.at[index, step],
-            )
-            for step in range(tp_size)
-        ])
-        for copy in arrivals[-1]:
-            copy.start()
-    grad = jnp.concatenate([grad_ref[step] for step in range(tp_size)], axis=1)
-    leaving = []
-    for index, (first, count) in enumerate(chunks):
-        for copy in arrivals[index]:
-            copy.wait()
-        out_buf[:, first:first + count] = dot(grad, w_buf[first:first + count, :], NT).astype(jnp.bfloat16)
-        leaving.append(
-            pltpu.make_async_copy(
-                out_buf.at[:, pl.ds(first, count)], out_ref.at[:, pl.ds(first, count)], out_sem.at[index]
-            )
-        )
-        leaving[-1].start()
-    for copy in leaving:
-        copy.wait()
-
-
-def scratch(tokens, heads, ctx_size, tp_size):
+def scratch(tokens, heads, features, ctx_size, tp_size):
     total_rows = tokens * ctx_size
     rows = tokens * heads
     chunk_rows = CHUNK_HEADS * tokens // 2
     far = ctx_size // 4
     block = (tokens, 2 * HEAD)
+    spread = spread_block(features, ctx_size)
+    share = (features - spread * ctx_size) // 2
     sems = pltpu.SemaphoreType.DMA
     return [
         pltpu.VMEM((rows, 4 * HEAD), jnp.bfloat16),
@@ -414,10 +466,17 @@
         pltpu.VMEM((far,) + block, jnp.bfloat16),
         pltpu.VMEM((far,) + block, jnp.bfloat16),
         pltpu.VMEM((far,) + block, jnp.bfloat16),
+        pltpu.VMEM((tp_size,) + block, jnp.bfloat16),
+        pltpu.VMEM((tp_size, features, 2 * HEAD), jnp.bfloat16),
+        pltpu.VMEM((tp_size - 1, spread + share, 2 * HEAD), jnp.bfloat16),
+        pltpu.VMEM((tokens, features), jnp.bfloat16),
         sems((far,)), sems((far,)), sems((far,)), sems((far,)), sems((far, 2)), sems((far, 2)),
         sems((2 * far,)), sems((2 * far,)), sems((far,)), sems((far,)), sems((far,)), sems((far,)),
         sems((tp_size, 4)), sems((tp_size, 4)), sems((tp_size, 4)), sems((tp_size, 4)), sems(()),
         sems((tp_size,)), sems((tp_size,)),
+        sems((tp_size, 2)), sems((tp_size,)), sems((tp_size,)), sems((tp_size, far)), sems((tp_size, far)),
+        sems((tp_size, far)), sems((tp_size, far)), sems((tp_size, far, 2)), sems((tp_size, far, 2)),
+        sems((len(feature_chunks(features)),)),
     ]
 
 
@@ -429,35 +488,19 @@
     features = kv_weight.shape[0] // tp_size
     vmem = pl.BlockSpec(memory_space=pltpu.VMEM)
     anywhere = pl.BlockSpec(memory_space=pl.ANY)
-    query_grad, kv_grad, weights = pl.pallas_call(
+    return pl.pallas_call(
         functools.partial(backward_kernel, ctx_size, tp_size),
         out_shape=(
             jax.ShapeDtypeStruct(queries.shape, jnp.bfloat16),
-            jax.ShapeDtypeStruct((tp_size, tokens, 2 * HEAD), jnp.bfloat16),
-            jax.ShapeDtypeStruct((tp_size, features, 2 * HEAD), jnp.bfloat16),
+            jax.ShapeDtypeStruct((tokens, features), jnp.bfloat16),
         ),
         in_specs=[pl.BlockSpec(memory_space=pltpu.SMEM)] + [vmem] * 4 + [anywhere],
-        out_specs=(vmem, vmem, anywhere),
-        scratch_shapes=scratch(tokens, heads, ctx_size, tp_size),
+        out_specs=(vmem, anywhere),
+        scratch_shapes=scratch(tokens, heads, features, ctx_size, tp_size),
         compiler_params=pltpu.CompilerParams(
             vmem_limit_bytes=56 * 2**20, collective_id=0, has_side_effects=True
         ),
     )(span_table, queries, out_grad, forward_out, keys_values, kv_weight)
-    chunks = feature_chunks(features)
-    input_grad = pl.pallas_call(
-        functools.partial(project_kernel, chunks),
-        out_shape=jax.ShapeDtypeStruct((tokens, features), jnp.bfloat16),
-        in_specs=[vmem, anywhere],
-        out_specs=anywhere,
-        scratch_shapes=[
-            pltpu.VMEM((features, tp_size * 2 * HEAD), jnp.bfloat16),
-            pltpu.VMEM((tokens, features), jnp.bfloat16),
-            pltpu.SemaphoreType.DMA((len(chunks), tp_size)),
-            pltpu.SemaphoreType.DMA((len(chunks),)),
-        ],
-        compiler_params=pltpu.CompilerParams(vmem_limit_bytes=24 * 2**20),
-    )(kv_grad, weights)
-    return (query_grad, input_grad)
 
 
 def solution(mesh):

time: 74.9 us -> 54.5 us (0.73)
  Pallas kernels: 70.4 us -> 49.1 us
  local copies, waits for them, and re-layouts: 3.62 us -> 4.56 us
    pallas_call x1, Pallas kernels: 66.5 us -> 49.1 us  [on_device(): pl.pallas_call(functools.partial(backward_kernel, ctx_size, tp_size), out...]
    pallas_call x1 -> x0, Pallas kernels: 3.89 us -> none  [on_device(): pl.pallas_call(functools.partial(project_kernel, chunks), out_shape=jax.S...]
    unnamed x7 -> x2, local copies, waits for them, and re-layouts: 3.62 us -> 4.56 us
where the time goes in v4:
time: 54.5 us; the launch traced here: 54.3 us
  Pallas kernels  49.1 us (90%)
  local copies, waits for them, and re-layouts  4.56 us (8%)
  between operations  0.64 us (1%)
    pallas_call x1, Pallas kernels, on_device(): pl.pallas_call(functools.partial(backward_kernel, ctx_size, tp_size), out...  49.1 us
    unnamed x2, local copies, waits for them, and re-layouts  4.56 us

profile of v4, /device:TPU:0, one launch (start us, length us, event | category | flops | bytes accessed | tf_op | source)
XLA Modules:
  0.0 54.3 jit_solution(8419827119361306203)
XLA Ops:
  0.6 49.1 %shard_map.77 = (bf16[128,1024]{1,0:T(8,128)(2,1)}, bf16[128,7424]{1,0:T(8,128)(2,1)}) custom-call(s32[32]{0:T(128)} %table_ref.1, bf16[128,1024]{1,0:T(8,128)(2,1)} %q_ref.1, bf16[128,1024]{1,0:T(8,128)(2,1)} %do_ref.1, bf16[128,1024]{1,0:T(8,128)(2,1)} %fo_ref.1, bf16[128,128]{1,0:T(8,128)(2,1)} %kv_ref.1, bf16[14848,128]{1,0:T(8,128)(2,1)} %w_ref.1), custom_call_target="tpu_custom_call" | custom-call | tf_op jit(solution)/shard_map/pallas_call | solution.py:491
  49.8 1.7 %copy.10 = bf16[128,1024]{1,0:T(8,128)(2,1)} copy(bf16[128,1024]{1,0:T(8,128)(2,1)} %get-tuple-element.4) | data formatting | bytes 524288
  51.4 2.9 %copy.11 = bf16[128,7424]{1,0:T(8,128)(2,1)} copy(bf16[128,7424]{1,0:T(8,128)(2,1)} %get-tuple-element.5) | data formatting | bytes 3801088

commit v5 on v4

--- a/solution.py
+++ b/solution.py
@@ -82,7 +82,7 @@
         kx[half, at, 2 * HEAD:4 * HEAD] = jnp.where(wanted == col, 1.0, 0.0).astype(jnp.bfloat16)
 
 
-def attention(chunk_count, chunk_rows, total_rows, span_rows, kx, kt, vx, qx, qs, dox, dos, score, dkv, dq_ref, after_chunk, tile_order, after_tile):
+def attention(chunk_count, chunk_rows, total_rows, span_rows, kx, kt, vx, qx, qs, dox, dos, score, dkv, dq_ref, mid_chunk, after_chunk, tile_order, after_tile):
     tiles = total_rows // KEY_TILE
     heads = dq_ref.shape[1] // HEAD
 
@@ -120,6 +120,7 @@
                 top = score_tile(chunk + 1, tile, top)
             total = exp_tile(chunk, tile, peak, total)
         inverse = 1.0 / jnp.sum(total, axis=0, keepdims=True)
+        mid_chunk(chunk)
 
         def second(tile, dqt, chunk=chunk, inverse=inverse):
             at = tile_at(tile)
@@ -165,11 +166,11 @@
     table_ref, q_ref, do_ref, fo_ref, kv_ref, w_ref,
     dq_ref, out_ref,
     qx, qs, dox, dos, kx, kt, vx, score, dkv,
-    gathered, mate_sum, row_out, row_in, far_out, far_in, grad_ref, wall_ref, staged, out_buf,
+    gathered, mate_sum, row_out, row_in, far_out, far_in, grad_ref, wall_ref, staged,
     gz_send, gz_recv, gy_send, gy_recv, gm_send, gm_recv,
     rm_send, rm_recv, ry_send, ry_recv, rz_send, rz_recv,
     wx_send, wx_recv, wm_send, wm_recv, own_sem, t_send, t_recv,
-    stage_sem, bx_send, bx_recv, bz_send, bz_recv, by_send, by_recv, bm_send, bm_recv, out_sem,
+    stage_sem, bx_send, bx_recv, bz_send, bz_recv, by_send, by_recv, bm_send, bm_recv,
 ):
     tokens = q_ref.shape[0]
     total_rows = gathered.shape[0]
@@ -278,20 +279,28 @@
                 )
             block_to_mates(step, 0)
 
-    def spread_far_blocks():
+    def spread_far_block(hop):
         for step in range(1, tp_size):
-            for hop in range(1, far):
-                block_far[step, hop].wait_recv()
-                block_to_mates(step, hop)
-
-    def spread_row_blocks():
+            block_far[step, hop].wait_recv()
+            block_to_mates(step, hop)
+
+    def spread_row_block(hop):
         for step in range(1, tp_size):
-            for hop in range(far):
-                block_row[step, hop].wait_recv()
-                here = wall_block(step, place(behind(hop), 1 - mid, core))
-                block_core.append(
-                    send(here, here, bm_send.at[step, hop, 1], bm_recv.at[step, hop, 1], "ctx", core_mate)
-                )
+            block_row[step, hop].wait_recv()
+            here = wall_block(step, place(behind(hop), 1 - mid, core))
+            block_core.append(
+                send(here, here, bm_send.at[step, hop, 1], bm_recv.at[step, hop, 1], "ctx", core_mate)
+            )
+
+    tasks = [(spread_far_block, hop) for hop in range(1, far)]
+    tasks.insert(1, (spread_row_block, 0))
+    tasks += [(spread_row_block, hop) for hop in range(1, far)]
+    points = 6
+
+    def run_tasks(point):
+        for index, (task, hop) in enumerate(tasks):
+            if index * points // len(tasks) == point:
+                task(hop)
 
     first_span = me * 2
     spread_queries(table_ref, first_span, 0, q_ref, do_ref, fo_ref, qx, qs, dox, dos)
@@ -336,15 +345,19 @@
                 send(here, here, wm_send.at[step, piece], wm_recv.at[step, piece], "ctx", core_mate)
             )
 
+    chunk_rows = CHUNK_HEADS * tokens // 2
+    chunk_count = qx.shape[0] // chunk_rows
     spread_own_blocks()
 
     def after_chunk(chunk):
-        if chunk == 0:
-            spread_far_blocks()
-        if chunk == 1:
-            spread_row_blocks()
-        if chunk + 1 < chunk_count and chunk < pieces:
-            share_weights(chunk)
+        if chunk + 1 < chunk_count:
+            run_tasks(2 * chunk)
+            if chunk < pieces:
+                share_weights(chunk)
+
+    def mid_chunk(chunk):
+        if 1 <= chunk and chunk + 1 < chunk_count:
+            run_tasks(2 * chunk - 1)
 
     def turn_place(turn):
         return around(turn % far + 1), (1 - mid if turn < far else mid)
@@ -391,14 +404,13 @@
         if turn >= lag:
             pass_on(turn - lag)
 
-    chunk_rows = CHUNK_HEADS * tokens // 2
-    chunk_count = qx.shape[0] // chunk_rows
     attention(
         chunk_count, chunk_rows, total_rows, tokens // 2, kx, kt, vx, qx, qs, dox, dos, score, dkv, dq_ref,
-        after_chunk, tile_order, after_tile,
+        mid_chunk, after_chunk, tile_order, after_tile,
     )
     for turn in range(2 * far - lag, 2 * far):
         if turn + 1 == 2 * far:
+            run_tasks(points - 1)
             for piece in range(chunk_count - 1, pieces):
                 share_weights(piece)
         pass_on(turn)
@@ -414,20 +426,15 @@
         copy.wait_recv()
     own_copy.wait()
     grad = jnp.concatenate([grad_ref[step] for step in range(tp_size)], axis=1)
-    leaving = []
-    for index, (first, count) in enumerate(feature_chunks(features)):
+    for first, count in feature_chunks(features):
         at = pl.ds(first, count)
         weights = jnp.concatenate([wall_ref[step, at, :] for step in range(tp_size)], axis=1)
-        out_buf[:, at] = dot(grad, weights, NT).astype(jnp.bfloat16)
-        leaving.append(pltpu.make_async_copy(out_buf.at[:, at], out_ref.at[:, at], out_sem.at[index]))
-        leaving[-1].start()
+        out_ref[:, at] = dot(grad, weights, NT).astype(jnp.bfloat16)
     for copy in to_core + to_row + to_far + last + weight_mate + block_core:
         copy.wait_send()
     for copies in (weight_in, block_in, block_far, block_row):
         for copy in copies.values():
             copy.wait_send()
-    for copy in leaving:
-        copy.wait()
 
 
 def spread_block(features, ctx_size):
@@ -469,14 +476,12 @@
         pltpu.VMEM((tp_size,) + block, jnp.bfloat16),
         pltpu.VMEM((tp_size, features, 2 * HEAD), jnp.bfloat16),
         pltpu.VMEM((tp_size - 1, spread + share, 2 * HEAD), jnp.bfloat16),
-        pltpu.VMEM((tokens, features), jnp.bfloat16),
         sems((far,)), sems((far,)), sems((far,)), sems((far,)), sems((far, 2)), sems((far, 2)),
         sems((2 * far,)), sems((2 * far,)), sems((far,)), sems((far,)), sems((far,)), sems((far,)),
         sems((tp_size, 4)), sems((tp_size, 4)), sems((tp_size, 4)), sems((tp_size, 4)), sems(()),
         sems((tp_size,)), sems((tp_size,)),
         sems((tp_size, 2)), sems((tp_size,)), sems((tp_size,)), sems((tp_size, far)), sems((tp_size, far)),
         sems((tp_size, far)), sems((tp_size, far)), sems((tp_size, far, 2)), sems((tp_size, far, 2)),
-        sems((len(feature_chunks(features)),)),
     ]
 
 
@@ -495,10 +500,10 @@
             jax.ShapeDtypeStruct((tokens, features), jnp.bfloat16),
         ),
         in_specs=[pl.BlockSpec(memory_space=pltpu.SMEM)] + [vmem] * 4 + [anywhere],
-        out_specs=(vmem, anywhere),
+        out_specs=(vmem, vmem),
         scratch_shapes=scratch(tokens, heads, features, ctx_size, tp_size),
         compiler_params=pltpu.CompilerParams(
-            vmem_limit_bytes=56 * 2**20, collective_id=0, has_side_effects=True
+            vmem_limit_bytes=50 * 2**20, collective_id=0, has_side_effects=True
         ),
     )(span_table, queries, out_grad, forward_out, keys_values, kv_weight)
 

time: 54.5 us -> 52.4 us (0.961)
  Pallas kernels: 49.1 us -> 45.2 us
  local copies, waits for them, and re-layouts: 4.56 us -> 6.21 us
    pallas_call x1, Pallas kernels: 49.1 us -> 45.2 us  [on_device(): pl.pallas_call(functools.partial(backward_kernel, ctx_size, tp_size), out...]
    unnamed x2 -> x12, local copies, waits for them, and re-layouts: 4.56 us -> 6.21 us
where the time goes in v5:
time: 52.4 us; the launch traced here: 52.1 us
  Pallas kernels  45.2 us (86%)
  local copies, waits for them, and re-layouts  6.21 us (12%)
  between operations  0.65 us (1%)
    pallas_call x1, Pallas kernels, on_device(): pl.pallas_call(functools.partial(backward_kernel, ctx_size, tp_size), out...  45.2 us
    unnamed x12, local copies, waits for them, and re-layouts  6.21 us

profile of v5, /device:TPU:0, one launch (start us, length us, event | category | flops | bytes accessed | tf_op | source)
XLA Modules:
  0.0 52.1 jit_solution(4226307508036125956)
XLA Ops:
  0.6 0.0 copy-start
  0.6 0.9 %copy-done = bf16[128,1024]{1,0:T(8,128)(2,1)S(1)} copy-done((bf16[128,1024]{1,0:T(8,128)(2,1)S(1)}, bf16[128,1024]{1,0:T(8,128)(2,1)}, u32[]{:S(2)}) %copy-start) | copy-done | bytes 262168
  1.6 0.0 copy-start.1
  1.6 0.9 %copy-done.1 = bf16[128,1024]{1,0:T(8,128)(2,1)S(1)} copy-done((bf16[128,1024]{1,0:T(8,128)(2,1)S(1)}, bf16[128,1024]{1,0:T(8,128)(2,1)}, u32[]{:S(2)}) %copy-start.1) | copy-done | bytes 262168
  2.5 0.0 copy-start.2
  2.5 0.9 %copy-done.2 = bf16[128,1024]{1,0:T(8,128)(2,1)S(1)} copy-done((bf16[128,1024]{1,0:T(8,128)(2,1)S(1)}, bf16[128,1024]{1,0:T(8,128)(2,1)}, u32[]{:S(2)}) %copy-start.2) | copy-done | bytes 262168
  3.5 0.0 copy-start.3
  3.5 0.8 %copy-done.3 = bf16[128,128]{1,0:T(8,128)(2,1)S(1)} copy-done((bf16[128,128]{1,0:T(8,128)(2,1)S(1)}, bf16[128,128]{1,0:T(8,128)(2,1)}, u32[]{:S(2)}) %copy-start.3) | copy-done | bytes 32792
  4.2 0.0 copy-start.4
  4.2 0.7 %copy-done.4 = s32[32]{0:T(128)S(1)} copy-done((s32[32]{0:T(128)S(1)}, s32[32]{0:T(128)}, u32[]{:S(2)}) %copy-start.4) | copy-done | bytes 152
  4.9 45.2 %shard_map.77 = (bf16[128,1024]{1,0:T(8,128)(2,1)S(1)}, bf16[128,7424]{1,0:T(8,128)(2,1)S(1)}) custom-call(s32[32]{0:T(128)S(1)} %copy-done.4, bf16[128,1024]{1,0:T(8,128)(2,1)S(1)} %copy-done, bf16[128,1024]{1,0:T(8,128)(2,1)S(1)} %copy-done.1, bf16[128,1024]{1,0:T(8,128)(2,1)S(1)} %copy-done.2, bf16[128,128]{1,0:T(8,128)(2,1)S(1)} %copy-done.3, ...), custom_call_target="tpu_custom_call" | custom-call | tf_op jit(solution)/shard_map/pallas_call | solution.py:496
  50.1 0.7 %copy.10 = bf16[128,1024]{1,0:T(8,128)(2,1)} copy(bf16[128,1024]{1,0:T(8,128)(2,1)S(1)} %get-tuple-element.4) | data formatting | bytes 524288
  50.8 1.2 %copy.11 = bf16[128,7424]{1,0:T(8,128)(2,1)} copy(bf16[128,7424]{1,0:T(8,128)(2,1)S(1)} %get-tuple-element.5) | data formatting | bytes 3801088
Async XLA Ops:
  0.6 1.0 %copy-start = (bf16[128,1024]{1,0:T(8,128)(2,1)S(1)}, bf16[128,1024]{1,0:T(8,128)(2,1)}, u32[]{:S(2)}) copy-start(bf16[128,1024]{1,0:T(8,128)(2,1)} %q_ref.1) | copy-start | bytes 786436
  1.6 0.9 %copy-start.1 = (bf16[128,1024]{1,0:T(8,128)(2,1)S(1)}, bf16[128,1024]{1,0:T(8,128)(2,1)}, u32[]{:S(2)}) copy-start(bf16[128,1024]{1,0:T(8,128)(2,1)} %do_ref.1) | copy-start | bytes 786436
  2.5 0.9 %copy-start.2 = (bf16[128,1024]{1,0:T(8,128)(2,1)S(1)}, bf16[128,1024]{1,0:T(8,128)(2,1)}, u32[]{:S(2)}) copy-start(bf16[128,1024]{1,0:T(8,128)(2,1)} %fo_ref.1) | copy-start | bytes 786436
  3.5 0.8 %copy-start.3 = (bf16[128,128]{1,0:T(8,128)(2,1)S(1)}, bf16[128,128]{1,0:T(8,128)(2,1)}, u32[]{:S(2)}) copy-start(bf16[128,128]{1,0:T(8,128)(2,1)} %kv_ref.1) | copy-start | bytes 98308
  4.2 0.7 %copy-start.4 = (s32[32]{0:T(128)S(1)}, s32[32]{0:T(128)}, u32[]{:S(2)}) copy-start(s32[32]{0:T(128)} %table_ref.1) | copy-start | bytes 388
